TPU v7x, 32 devices: a whole 2x2x4 slice. The times are simulated.
32 devices in a mesh: pipe: 2 (over y), ctx: 8 (over z, x), tp: 2 (over core).
Axes of the slice: x: 2, y: 2, z: 4, core: 2. Of those that a mesh axis runs over, the one named last changes fastest.
Arguments:
- inputs: bfloat16 [2, 1024, 1536], P(None, ('ctx', 'tp')), may hold values from -6 to 6
- cotangent: bfloat16 [2, 1024, 1536], P(None, ('ctx', 'tp')), may hold values from -6 to 6
- norm_attn: float32 [2, 1536], P('pipe'), may hold values from 0.1 to 1.9
- w_query: bfloat16 [2, 1536, 1536], P('pipe', None, 'tp'), may hold values from -0.15625 to 0.15625
- w_key: bfloat16 [2, 1536, 768], P('pipe', None, 'tp'), may hold values from -0.15625 to 0.15625
- w_value: bfloat16 [2, 1536, 768], P('pipe', None, 'tp'), may hold values from -0.15625 to 0.15625
- w_out: bfloat16 [2, 1536, 1536], P('pipe', None, 'tp'), may hold values from -2 to 2
- norm_mlp: float32 [2, 1536], P('pipe'), may hold values from 0.1 to 1.9
- w_gate: bfloat16 [2, 1536, 4096], P('pipe', None, 'tp'), may hold values from -0.15625 to 0.15625
- w_up: bfloat16 [2, 1536, 4096], P('pipe', None, 'tp'), may hold values from -0.15625 to 0.15625
- w_down: bfloat16 [2, 1536, 4096], P('pipe', None, 'tp'), may hold values from -0.09375 to 0.09375
Outputs:
- section_outputs: bfloat16 [2, 2, 1024, 1536], P('pipe', None, ('ctx', 'tp'))
- input_grads: float32 [2, 2, 1024, 1536], P('pipe', None, ('ctx', 'tp'))
- grad_norm_attn: float32 [2, 1536], P('pipe', 'ctx')
- grad_query: float32 [2, 1536, 1536], P('pipe', 'ctx', 'tp')
- grad_key: float32 [2, 1536, 768], P('pipe', 'ctx', 'tp')
- grad_value: float32 [2, 1536, 768], P('pipe', 'ctx', 'tp')
- grad_out: float32 [2, 1536, 1536], P('pipe', 'ctx', 'tp')
- grad_norm_mlp: float32 [2, 1536], P('pipe', 'ctx')
- grad_gate: float32 [2, 1536, 4096], P('pipe', 'ctx', 'tp')
- grad_up: float32 [2, 1536, 4096], P('pipe', 'ctx', 'tp')
- grad_down: float32 [2, 1536, 4096], P('pipe', 'ctx', 'tp')
All inputs are finite; a program needn't handle non-finite values.
Results may differ from a plain program's by a relative error of at most 0.03.
Values may be sent and summed in bfloat16 or wider, within the bound.
No kernel may reach another device: no remote copies, remote signals or barrier semaphores. Data moves between devices by JAX's collectives and lax.ppermute only.
A program may use at most 256 MiB of HBM per device.

v0:
```python
import jax
import jax.numpy as jnp
from jax import lax
from jax.sharding import PartitionSpec as P

HD = 96


epsilon = 1e-05
base_theta = 100000.0


def shifted(array, axis, by):
    size = lax.axis_size(axis)
    pairs = [(i, i + by) for i in range(size) if 0 <= i + by < size]
    return lax.ppermute(array, axis, pairs)


def place_rows(row_ids, half_rows, halves):
    block_id = row_ids // half_rows
    pair_id = block_id // 2
    pos_block = jnp.where(block_id % 2 == 0, pair_id, halves - 1 - pair_id)
    return pos_block * half_rows + row_ids % half_rows


def rotary_tables(positions):
    frequency = base_theta ** (-jnp.arange(0, HD, 2).astype(jnp.float32) / HD)
    angles = positions.astype(jnp.float32)[:, None] * frequency[None, :]
    angles = jnp.concatenate([angles, angles], axis=1)
    return (jnp.cos(angles), jnp.sin(angles))


def rotate(values, cosine, sine_tab, sign_val):
    half_dim = values.shape[-1] // 2
    swapped = jnp.concatenate([-values[..., half_dim:], values[..., :half_dim]], axis=-1)
    return values * cosine[:, None, :] + sign_val * swapped * sine_tab[:, None, :]


def normalize(values, gain_vec):
    inv_scale = lax.rsqrt(jnp.mean(values * values, axis=-1, keepdims=True) + epsilon)
    normed = values * inv_scale
    return (normed * gain_vec, normed, inv_scale)


def norm_back(upstream, normed, inv_scale, gain_vec):
    scaled = upstream * gain_vec
    down_grad = inv_scale * (scaled - normed * jnp.mean(scaled * normed, axis=-1, keepdims=True))
    return (down_grad, jnp.sum(upstream * normed, axis=0))


def dot_plain(left_op, right_op):
    return jnp.dot(left_op, right_op, preferred_element_type=jnp.float32)


def dot_right_t(left_op, right_op):
    return lax.dot_general(
        left_op, right_op, (((1,), (1,)), ((), ())), preferred_element_type=jnp.float32
    )


def dot_left_t(left_op, right_op):
    return lax.dot_general(
        left_op, right_op, (((0,), (0,)), ((), ())), preferred_element_type=jnp.float32
    )


def score_block(queries, keys_part, query_pos, key_pos, groups):
    query_count = queries.shape[0]
    key_count = keys_part.shape[0]
    query4 = queries.reshape(query_count, groups, -1, HD)
    key_rows3 = keys_part.reshape(key_count, groups, HD)
    scores = jnp.einsum(
        "qgrd,kgd->grqk", query4, key_rows3, preferred_element_type=jnp.float32
    ) * HD ** (-0.5)
    return (scores, query_pos[:, None] >= key_pos[None, :])


def reduce_grads(grad_set):
    return (
        lax.psum_scatter(
            grad_set[0].astype(jnp.bfloat16), "ctx", scatter_dimension=0, tiled=True
        ).astype(jnp.float32),
        lax.psum_scatter(
            grad_set[1].astype(jnp.bfloat16), "ctx", scatter_dimension=0, tiled=True
        ).astype(jnp.float32),
        lax.psum_scatter(
            grad_set[2].astype(jnp.bfloat16), "ctx", scatter_dimension=0, tiled=True
        ).astype(jnp.float32),
        lax.psum_scatter(
            grad_set[3].astype(jnp.bfloat16), "ctx", scatter_dimension=0, tiled=True
        ).astype(jnp.float32),
        lax.psum_scatter(
            grad_set[4].astype(jnp.bfloat16), "ctx", scatter_dimension=0, tiled=True
        ).astype(jnp.float32),
        lax.psum_scatter(
            grad_set[5].astype(jnp.bfloat16), "ctx", scatter_dimension=0, tiled=True
        ).astype(jnp.float32),
        lax.psum_scatter(
            grad_set[6].astype(jnp.bfloat16), "ctx", scatter_dimension=0, tiled=True
        ).astype(jnp.float32),
        lax.psum_scatter(
            grad_set[7].astype(jnp.bfloat16), "ctx", scatter_dimension=0, tiled=True
        ).astype(jnp.float32),
        lax.psum_scatter(
            grad_set[8].astype(jnp.bfloat16), "ctx", scatter_dimension=0, tiled=True
        ).astype(jnp.float32),
    )


def on_device(
    inputs, cotangent, norm_attn, w_query, w_key, w_value, w_out, norm_mlp, w_gate, w_up, w_down
):
    params = (
        norm_attn[0],
        w_query[0],
        w_key[0],
        w_value[0],
        w_out[0],
        norm_mlp[0],
        w_gate[0],
        w_up[0],
        w_down[0],
    )
    gain_attn, query_w, key_w, value_w, out_w, gain_mlp, gate_w, up_w, down_w = params
    batches, local_rows, model_width = inputs.shape
    span_rows = local_rows * lax.axis_size("tp")
    seq_len = span_rows * lax.axis_size("ctx")
    half_rows = span_rows // 2
    halves = 2 * lax.axis_size("ctx")
    groups = key_w.shape[1] // HD
    head_count = query_w.shape[1] // HD
    repeat = head_count // groups
    kv_width = groups * HD
    section_at = lax.axis_index("pipe")
    sections = lax.axis_size("pipe")
    ctx_at = lax.axis_index("ctx")
    own_pos = place_rows(
        ctx_at * span_rows + jnp.arange(span_rows, dtype=jnp.int32), half_rows, halves
    )
    all_pos = place_rows(jnp.arange(seq_len, dtype=jnp.int32), half_rows, halves)
    cosine, sine_tab = rotary_tables(own_pos)
    kept_bufs = None
    section_out = jnp.zeros((batches, local_rows, model_width), jnp.bfloat16)
    outgoing = jnp.zeros((local_rows, model_width), jnp.bfloat16)
    for tick_at in range(batches + sections - 1):
        arrived = shifted(outgoing, "pipe", 1)
        slot_raw = tick_at - section_at
        is_live = (slot_raw >= 0) & (slot_raw < batches)
        slot_at = jnp.clip(slot_raw, 0, batches - 1)
        section_in = jnp.where(section_at == 0, inputs[min(tick_at, batches - 1)], arrived).astype(
            jnp.float32
        )
        normed_attn = normalize(section_in, gain_attn)[0]
        forward_attn_full = lax.all_gather(
            normed_attn.astype(jnp.bfloat16), "tp", axis=0, tiled=True
        )
        forward_queries = rotate(
            dot_plain(forward_attn_full, query_w).reshape(span_rows, head_count, HD),
            cosine,
            sine_tab,
            1.0,
        )
        forward_queries = forward_queries.reshape(span_rows, head_count * HD).astype(jnp.bfloat16)
        keys_own = rotate(
            dot_plain(forward_attn_full, key_w).reshape(span_rows, groups, HD),
            cosine,
            sine_tab,
            1.0,
        )
        keys_own = keys_own.reshape(span_rows, kv_width).astype(jnp.bfloat16)
        values_own = dot_plain(forward_attn_full, value_w).astype(jnp.bfloat16)
        forward_keys_all = lax.all_gather(keys_own, "ctx", axis=0, tiled=True)
        forward_values_all = lax.all_gather(values_own, "ctx", axis=0, tiled=True)
        forward_scores, forward_allowed = score_block(
            forward_queries, forward_keys_all, own_pos, all_pos, groups
        )
        forward_scores = jnp.where(forward_allowed, forward_scores, -jnp.inf)
        top_score = jnp.max(forward_scores, axis=-1, keepdims=True)
        exp_scores = jnp.exp(forward_scores - top_score)
        totals = jnp.sum(exp_scores, axis=-1, keepdims=True)
        forward_prob_low = (exp_scores / totals).astype(jnp.bfloat16)
        mixed4 = jnp.einsum(
            "grqk,kgd->qgrd",
            forward_prob_low,
            forward_values_all.reshape(seq_len, groups, HD),
            preferred_element_type=jnp.float32,
        )
        forward_mixed_out = mixed4.reshape(span_rows, head_count * HD).astype(jnp.bfloat16)
        forward_log_total = top_score[..., 0] + jnp.log(totals[..., 0])
        forward_middle = section_in + lax.psum_scatter(
            dot_right_t(forward_mixed_out, out_w).astype(jnp.bfloat16),
            "tp",
            scatter_dimension=0,
            tiled=True,
        ).astype(jnp.float32)
        normed_mlp = normalize(forward_middle, gain_mlp)[0]
        forward_mlp_full = lax.all_gather(normed_mlp.astype(jnp.bfloat16), "tp", axis=0, tiled=True)
        forward_gate_pre = dot_plain(forward_mlp_full, gate_w)
        forward_up_pre = dot_plain(forward_mlp_full, up_w)
        forward_inner_act = (
            forward_gate_pre * jax.nn.sigmoid(forward_gate_pre) * forward_up_pre
        ).astype(jnp.bfloat16)
        result = forward_middle + lax.psum_scatter(
            dot_right_t(forward_inner_act, down_w).astype(jnp.bfloat16),
            "tp",
            scatter_dimension=0,
            tiled=True,
        ).astype(jnp.float32)
        forward_kept_acts = (
            section_in,
            forward_attn_full,
            forward_queries,
            forward_keys_all,
            forward_values_all,
            forward_mixed_out,
            forward_log_total,
            forward_middle,
            forward_mlp_full,
            forward_gate_pre,
            forward_up_pre,
        )
        result, kept_acts = (result, forward_kept_acts)
        if kept_bufs is None:
            kept_bufs = tuple(
                (
                    jnp.zeros((batches,) + piece_act.shape, piece_act.dtype)
                    for piece_act in kept_acts
                )
            )
        kept_bufs = tuple(
            (
                jnp.where(is_live, buffer.at[slot_at].set(piece_act), buffer)
                for buffer, piece_act in zip(kept_bufs, kept_acts)
            )
        )
        outgoing = result.astype(jnp.bfloat16)
        section_out = jnp.where(is_live, section_out.at[slot_at].set(outgoing), section_out)
    input_grads = jnp.zeros((batches, local_rows, model_width), jnp.float32)
    grad_acc = tuple((jnp.zeros(weight.shape, jnp.float32) for weight in params))
    outgoing = jnp.zeros((local_rows, model_width), jnp.bfloat16)
    for tick_at in range(batches + sections - 1):
        arrived = shifted(outgoing, "pipe", -1)
        slot_raw = tick_at - (sections - 1 - section_at)
        is_live = (slot_raw >= 0) & (slot_raw < batches)
        slot_at = jnp.clip(slot_raw, 0, batches - 1)
        upstream = jnp.where(
            section_at == sections - 1,
            cotangent[slot_at].astype(jnp.float32),
            arrived.astype(jnp.float32),
        )
        (
            hidden_in,
            attn_full,
            queries,
            keys_all,
            values_all,
            mixed_out,
            log_total,
            middle,
            mlp_full,
            gate_pre,
            up_pre,
        ) = tuple((buffer[slot_at] for buffer in kept_bufs))
        branch_full = lax.all_gather(upstream.astype(jnp.bfloat16), "tp", axis=0, tiled=True)
        sigmoid_g = jax.nn.sigmoid(gate_pre)
        silu_gate = gate_pre * sigmoid_g
        inner_act = (silu_gate * up_pre).astype(jnp.bfloat16)
        grad_down = dot_left_t(branch_full, inner_act)
        inner_grad = dot_plain(branch_full, down_w)
        gate_grad = (inner_grad * up_pre * sigmoid_g * (1.0 + gate_pre * (1.0 - sigmoid_g))).astype(
            jnp.bfloat16
        )
        up_grad = (inner_grad * silu_gate).astype(jnp.bfloat16)
        grad_gate = dot_left_t(mlp_full, gate_grad)
        grad_up = dot_left_t(mlp_full, up_grad)
        normed_grad = lax.psum_scatter(
            (dot_right_t(gate_grad, gate_w) + dot_right_t(up_grad, up_w)).astype(jnp.bfloat16),
            "tp",
            scatter_dimension=0,
            tiled=True,
        ).astype(jnp.float32)
        second_norm = normalize(middle, gain_mlp)
        middle_norm_grad, grad_gain_mlp = norm_back(
            normed_grad, second_norm[1], second_norm[2], gain_mlp
        )
        middle_grad = upstream + middle_norm_grad
        attn_out_full = lax.all_gather(middle_grad.astype(jnp.bfloat16), "tp", axis=0, tiled=True)
        grad_out = dot_left_t(attn_out_full, mixed_out)
        mixed_grad = dot_plain(attn_out_full, out_w).astype(jnp.bfloat16)
        scores, allowed = score_block(queries, keys_all, own_pos, all_pos, groups)
        prob_f32 = jnp.where(allowed, jnp.exp(scores - log_total[..., None]), 0.0)
        grad_rows4 = mixed_grad.reshape(span_rows, groups, repeat, HD)
        prob_grad = jnp.einsum(
            "qgrd,kgd->grqk",
            grad_rows4,
            values_all.reshape(seq_len, groups, HD),
            preferred_element_type=jnp.float32,
        )
        inner_sum = jnp.sum(prob_f32 * prob_grad, axis=-1, keepdims=True)
        score_grad = (prob_f32 * (prob_grad - inner_sum)).astype(jnp.bfloat16)
        prob_low = prob_f32.astype(jnp.bfloat16)
        query_grad4 = jnp.einsum(
            "grqk,kgd->qgrd",
            score_grad,
            keys_all.reshape(seq_len, groups, HD),
            preferred_element_type=jnp.float32,
        ) * HD ** (-0.5)
        query4 = queries.reshape(span_rows, groups, repeat, HD)
        key_part = jnp.einsum(
            "grqk,qgrd->kgd", score_grad, query4, preferred_element_type=jnp.float32
        ) * HD ** (-0.5)
        value_part = jnp.einsum(
            "grqk,qgrd->kgd", prob_low, grad_rows4, preferred_element_type=jnp.float32
        )
        key_value_grad = lax.psum_scatter(
            jnp.concatenate(
                [
                    key_part.reshape(span_rows * lax.axis_size("ctx"), kv_width),
                    value_part.reshape(span_rows * lax.axis_size("ctx"), kv_width),
                ],
                axis=1,
            ).astype(jnp.bfloat16),
            "ctx",
            scatter_dimension=0,
            tiled=True,
        ).astype(jnp.float32)
        key_sum = key_value_grad[:, :kv_width]
        value_sum = key_value_grad[:, kv_width:]
        query_grad = rotate(query_grad4.reshape(span_rows, head_count, HD), cosine, sine_tab, -1.0)
        query_grad = query_grad.reshape(span_rows, head_count * HD).astype(jnp.bfloat16)
        key_grad = rotate(key_sum.reshape(span_rows, groups, HD), cosine, sine_tab, -1.0)
        key_grad = key_grad.reshape(span_rows, kv_width).astype(jnp.bfloat16)
        value_grad = value_sum.astype(jnp.bfloat16)
        grad_query = dot_left_t(attn_full, query_grad)
        grad_key = dot_left_t(attn_full, key_grad)
        grad_value = dot_left_t(attn_full, value_grad)
        total_q = dot_right_t(query_grad, query_w)
        total_k = dot_right_t(key_grad, key_w)
        attn_grad = lax.psum_scatter(
            (total_q + total_k + dot_right_t(value_grad, value_w)).astype(jnp.bfloat16),
            "tp",
            scatter_dimension=0,
            tiled=True,
        ).astype(jnp.float32)
        first_norm = normalize(hidden_in, gain_attn)
        input_norm_grad, grad_gain_attn = norm_back(
            attn_grad, first_norm[1], first_norm[2], gain_attn
        )
        grad_set = (
            grad_gain_attn,
            grad_query,
            grad_key,
            grad_value,
            grad_out,
            grad_gain_mlp,
            grad_gate,
            grad_up,
            grad_down,
        )
        down_grad, grad_set = (middle_grad + input_norm_grad, grad_set)
        outgoing = down_grad.astype(jnp.bfloat16)
        input_grads = jnp.where(is_live, input_grads.at[slot_at].set(down_grad), input_grads)
        masked = tuple((jnp.where(is_live, grad_one, 0.0) for grad_one in grad_set))
        grad_acc = tuple((acc_one + new_one for acc_one, new_one in zip(grad_acc, masked)))
    summed = reduce_grads(grad_acc)
    gain_one, gain_two = lax.psum((summed[0], summed[5]), "tp")
    return (
        section_out[None],
        input_grads[None],
        gain_one[None],
        summed[1][None],
        summed[2][None],
        summed[3][None],
        summed[4][None],
        gain_two[None],
        summed[6][None],
        summed[7][None],
        summed[8][None],
    )


def solution(mesh):
    placed = (
        P(None, ("ctx", "tp"), None),
        P(None, ("ctx", "tp"), None),
        P("pipe", None),
        P("pipe", None, "tp"),
        P("pipe", None, "tp"),
        P("pipe", None, "tp"),
        P("pipe", None, "tp"),
        P("pipe", None),
        P("pipe", None, "tp"),
        P("pipe", None, "tp"),
        P("pipe", None, "tp"),
    )
    return jax.shard_map(
        on_device,
        mesh=mesh,
        in_specs=placed,
        out_specs=(
            P("pipe", None, ("ctx", "tp"), None),
            P("pipe", None, ("ctx", "tp"), None),
            P("pipe", "ctx"),
            P("pipe", "ctx", "tp"),
            P("pipe", "ctx", "tp"),
            P("pipe", "ctx", "tp"),
            P("pipe", "ctx", "tp"),
            P("pipe", "ctx"),
            P("pipe", "ctx", "tp"),
            P("pipe", "ctx", "tp"),
            P("pipe", "ctx", "tp"),
        ),
        check_vma=False,
    )
```

profile of v0, /device:TPU:0, one launch (start us, length us, event | category | flops | bytes accessed | tf_op | source)
XLA Modules:
  0.0 1509.9 jit_solution(7155614579140627875)
XLA Ops:
  28.3 34.3 %all_gather.55 = bf16[1024,384]{1,0:T(8,128)(2,1)} all-gather(bf16[128,384]{1,0:T(8,128)(2,1)S(1)} %fusion.165), channel_id=1, replica_groups=mesh['pipe'=2,'ctx'=8,'tp'=2] {'ctx'}, dimensions={0}, use_global_device_ids=true | all-gather | bytes 884736 | tf_op jit(solution)/shard_map/all_gather | solution.py:173
  69.9 34.3 %all_gather.56 = bf16[1024,384]{1,0:T(8,128)(2,1)} all-gather(bf16[128,384]{1,0:T(8,128)(2,1)} %copy.89), channel_id=1, replica_groups=mesh['pipe'=2,'ctx'=8,'tp'=2] {'ctx'}, dimensions={0}, use_global_device_ids=true | all-gather | bytes 884736 | tf_op jit(solution)/shard_map/all_gather | solution.py:172
  172.0 34.2 %all_gather.59 = bf16[1024,384]{1,0:T(8,128)(2,1)} all-gather(bf16[128,384]{1,0:T(8,128)(2,1)S(1)} %fusion.168), channel_id=1, replica_groups=mesh['pipe'=2,'ctx'=8,'tp'=2] {'ctx'}, dimensions={0}, use_global_device_ids=true | all-gather | bytes 884736 | tf_op jit(solution)/shard_map/all_gather | solution.py:173
  212.6 34.3 %all_gather.60 = bf16[1024,384]{1,0:T(8,128)(2,1)} all-gather(bf16[128,384]{1,0:T(8,128)(2,1)} %copy.94), channel_id=1, replica_groups=mesh['pipe'=2,'ctx'=8,'tp'=2] {'ctx'}, dimensions={0}, use_global_device_ids=true | all-gather | bytes 884736 | tf_op jit(solution)/shard_map/all_gather | solution.py:172
  317.1 33.8 %all_gather.63 = bf16[1024,384]{1,0:T(8,128)(2,1)} all-gather(bf16[128,384]{1,0:T(8,128)(2,1)S(1)} %fusion.171), channel_id=1, replica_groups=mesh['pipe'=2,'ctx'=8,'tp'=2] {'ctx'}, dimensions={0}, use_global_device_ids=true | all-gather | bytes 884736 | tf_op jit(solution)/shard_map/all_gather | solution.py:173
  357.4 34.6 %all_gather.64 = bf16[1024,384]{1,0:T(8,128)(2,1)} all-gather(bf16[128,384]{1,0:T(8,128)(2,1)} %copy.98), channel_id=1, replica_groups=mesh['pipe'=2,'ctx'=8,'tp'=2] {'ctx'}, dimensions={0}, use_global_device_ids=true | all-gather | bytes 884736 | tf_op jit(solution)/shard_map/all_gather | solution.py:172
  492.0 60.8 %reduce-scatter.67.cloned.1.call-done = bf16[128,768]{1,0:T(8,128)(2,1)} async-done(((bf16[1024,768]{1,0:T(8,128)(2,1)}), bf16[128,768]{1,0:T(8,128)(2,1)}) %reduce-scatter.67.cloned.1.call-update) | async-done | bytes 196624
  570.5 7.6 collective-permute-done.4
  634.0 60.7 %reduce-scatter.69.cloned.1.call-done = bf16[128,768]{1,0:T(8,128)(2,1)} async-done(((bf16[1024,768]{1,0:T(8,128)(2,1)}), bf16[128,768]{1,0:T(8,128)(2,1)}) %reduce-scatter.69.cloned.1.call-update) | async-done | bytes 196624
  792.6 43.7 %reduce-scatter.71.cloned.1.call-done = bf16[128,768]{1,0:T(8,128)(2,1)} async-done(((bf16[1024,768]{1,0:T(8,128)(2,1)}), bf16[128,768]{1,0:T(8,128)(2,1)}) %reduce-scatter.71.cloned.1.call-update) | async-done | bytes 196624
  877.4 7.6 fusion.288
  892.4 7.9 add_convert_fusion.2
  900.4 7.6 fusion.286
  915.4 7.8 add_convert_fusion.1
  924.2 8.1 fusion.206
  932.4 7.7 fusion.208
  940.1 8.1 add_convert_fusion
  964.3 20.7 %all-reduce.3 = (bf16[1536]{0:T(1024)(128)(2,1)S(1)}, bf16[1536]{0:T(1024)(128)(2,1)}) all-reduce(bf16[1536]{0:T(1024)(128)(2,1)S(1)} %add_convert_fusion.12, bf16[1536]{0:T(1024)(128)(2,1)} %add_convert_fusion.11), channel_id=17, replica_groups=mesh['pipe'=2,'ctx'=8,'tp'=2] {'ctx'}, use_global_device_ids=true, to_apply=%region_54.55.clone | all-reduce | flops 3072 | bytes 12288
  993.9 8.1 reduce-scatter.59.cloned.1.call-done
  1003.9 65.7 %reduce-scatter.55.cloned.1.call-done = bf16[192,384]{1,0:T(8,128)(2,1)} async-done(((bf16[1536,384]{1,0:T(8,128)(2,1)}), bf16[192,384]{1,0:T(8,128)(2,1)}) %reduce-scatter.55.cloned.1.call-update) | async-done | bytes 147472 | tf_op jit(solution)/shard_map/reduce_scatter | solution.py:86
  1071.2 65.8 %reduce-scatter.57.cloned.1.call-done = bf16[192,384]{1,0:T(8,128)(2,1)} async-done(((bf16[1536,384]{1,0:T(8,128)(2,1)}), bf16[192,384]{1,0:T(8,128)(2,1)}) %reduce-scatter.57.cloned.1.call-update) | async-done | bytes 147472 | tf_op jit(solution)/shard_map/reduce_scatter | solution.py:89
  1138.7 119.2 %reduce-scatter.61.cloned.1.call-done = bf16[192,2048]{1,0:T(8,128)(2,1)} async-done(((bf16[1536,2048]{1,0:T(8,128)(2,1)}), bf16[192,2048]{1,0:T(8,128)(2,1)}) %reduce-scatter.61.cloned.1.call-update) | async-done | bytes 786448 | tf_op jit(solution)/shard_map/reduce_scatter | solution.py:98
  1260.3 118.7 %reduce-scatter.63.cloned.1.call-done = bf16[192,2048]{1,0:T(8,128)(2,1)} async-done(((bf16[1536,2048]{1,0:T(8,128)(2,1)}), bf16[192,2048]{1,0:T(8,128)(2,1)}) %reduce-scatter.63.cloned.1.call-update) | async-done | bytes 786448 | tf_op jit(solution)/shard_map/reduce_scatter | solution.py:101
  1381.4 118.7 %reduce-scatter.65.cloned.1.call-done = bf16[192,2048]{1,0:T(8,128)(2,1)} async-done(((bf16[1536,2048]{1,0:T(8,128)(2,1)}), bf16[192,2048]{1,0:T(8,128)(2,1)}) %reduce-scatter.65.cloned.1.call-update) | async-done | bytes 786448 | tf_op jit(solution)/shard_map/reduce_scatter | solution.py:104
  (622 shorter events, 542.4 us)
Async XLA Ops:
  7.2 118.9 %reduce-scatter.29.cloned.1.call-start = ((), (), s32[]{:S(2)}) async-start(), calls=%async_computation.22 | async-start | bytes 589824 | tf_op jit(solution)/shard_map/reduce_scatter | solution.py:190
  7.3 13.8 collective-permute-start
  117.4 35.6 %reduce-scatter.31.cloned.1.call-start = ((), (), s32[]{:S(2)}) async-start(), calls=%async_computation.23 | async-start | bytes 589824 | tf_op jit(solution)/shard_map/reduce_scatter | solution.py:203
  117.5 33.3 %collective-permute-start.3 = (bf16[64,1536]{1,0:T(8,128)(2,1)}, bf16[64,1536]{1,0:T(8,128)(2,1)}, u32[]{:S(2)}, u32[]{:S(2)}) collective-permute-start(bf16[64,1536]{1,0:T(8,128)(2,1)} %copy-done.105), channel_id=1, source_target_pairs={{16,0},{17,1},{18,2},{19,3},{20,4},{21,5},{22,6},{23,7},{24,8},{25... | collective-permute-start | bytes 589832 | tf_op jit(solution)/shard_map/ppermute | solution.py:16
  143.9 125.2 %reduce-scatter.33.cloned.1.call-start = ((), (), s32[]{:S(2)}) async-start(), calls=%async_computation.24 | async-start | bytes 589824 | tf_op jit(solution)/shard_map/reduce_scatter | solution.py:190
  258.5 40.1 %reduce-scatter.35.cloned.1.call-start = ((), (), s32[]{:S(2)}) async-start(), calls=%async_computation.25 | async-start | bytes 589824 | tf_op jit(solution)/shard_map/reduce_scatter | solution.py:203
  288.3 139.6 %reduce-scatter.37.cloned.1.call-start = ((), (), s32[]{:S(2)}) async-start(), calls=%async_computation.26 | async-start | bytes 589824 | tf_op jit(solution)/shard_map/reduce_scatter | solution.py:190
  403.6 62.3 %reduce-scatter.41.cloned.1.call-start = ((), (), s32[]{:S(2)}) async-start(), calls=%async_computation.28 | async-start | bytes 589824 | tf_op jit(solution)/shard_map/reduce_scatter | solution.py:276
  455.1 97.7 %reduce-scatter.67.cloned.1.call-start = ((), (), s32[]{:S(2)}) async-start(), calls=%async_computation.41 | async-start | bytes 1769472
  486.7 79.6 %reduce-scatter.43.cloned.1.call-start = ((), (), s32[]{:S(2)}) async-start(), calls=%async_computation.29 | async-start | bytes 589824 | tf_op jit(solution)/shard_map/reduce_scatter | solution.py:339
  559.4 47.0 %reduce-scatter.45.cloned.1.call-start = ((), (), s32[]{:S(2)}) async-start(), calls=%async_computation.30 | async-start | bytes 589824 | tf_op jit(solution)/shard_map/reduce_scatter | solution.py:276
  597.9 96.9 %reduce-scatter.69.cloned.1.call-start = ((), (), s32[]{:S(2)}) async-start(), calls=%async_computation.42 | async-start | bytes 1769472
  628.9 79.4 %reduce-scatter.47.cloned.1.call-start = ((), (), s32[]{:S(2)}) async-start(), calls=%async_computation.31 | async-start | bytes 589824 | tf_op jit(solution)/shard_map/reduce_scatter | solution.py:339
  701.4 47.2 %reduce-scatter.49.cloned.1.call-start = ((), (), s32[]{:S(2)}) async-start(), calls=%async_computation.32 | async-start | bytes 589824 | tf_op jit(solution)/shard_map/reduce_scatter | solution.py:276
  739.9 96.4 %reduce-scatter.71.cloned.1.call-start = ((), (), s32[]{:S(2)}) async-start(), calls=%async_computation.43 | async-start | bytes 1769472
  770.6 181.4 %reduce-scatter.39.cloned.1.call-start = ((), (), s32[]{:S(2)}) async-start(), calls=%async_computation.27 | async-start | bytes 589824 | tf_op jit(solution)/shard_map/reduce_scatter | solution.py:203
  784.8 177.1 %reduce-scatter.51.cloned.1.call-start = ((), (), s32[]{:S(2)}) async-start(), calls=%async_computation.33 | async-start | bytes 589824 | tf_op jit(solution)/shard_map/reduce_scatter | solution.py:339
  843.0 149.1 %reduce-scatter.53.cloned.1.call-start = ((), (), s32[]{:S(2)}) async-start(), calls=%async_computation.34 | async-start | bytes 2654208 | tf_op jit(solution)/shard_map/reduce_scatter | solution.py:83
  848.6 153.4 %reduce-scatter.59.cloned.1.call-start = ((), (), s32[]{:S(2)}) async-start(), calls=%async_computation.37 | async-start | bytes 2654208 | tf_op jit(solution)/shard_map/reduce_scatter | solution.py:92
  857.1 212.5 %reduce-scatter.55.cloned.1.call-start = ((), (), s32[]{:S(2)}) async-start(), calls=%async_computation.35 | async-start | bytes 1327104 | tf_op jit(solution)/shard_map/reduce_scatter | solution.py:86
  862.9 274.2 %reduce-scatter.57.cloned.1.call-start = ((), (), s32[]{:S(2)}) async-start(), calls=%async_computation.36 | async-start | bytes 1327104 | tf_op jit(solution)/shard_map/reduce_scatter | solution.py:89
  877.1 380.8 %reduce-scatter.61.cloned.1.call-start = ((), (), s32[]{:S(2)}) async-start(), calls=%async_computation.38 | async-start | bytes 7077888 | tf_op jit(solution)/shard_map/reduce_scatter | solution.py:98
  900.3 478.7 %reduce-scatter.63.cloned.1.call-start = ((), (), s32[]{:S(2)}) async-start(), calls=%async_computation.39 | async-start | bytes 7077888 | tf_op jit(solution)/shard_map/reduce_scatter | solution.py:101
  923.2 576.9 %reduce-scatter.65.cloned.1.call-start = ((), (), s32[]{:S(2)}) async-start(), calls=%async_computation.40 | async-start | bytes 7077888 | tf_op jit(solution)/shard_map/reduce_scatter | solution.py:104
  (135 other events, 2024.7 us)
Sparse Core Ops, SparseCore 0:
  117.6 8.4 reduce-scatter.28
  144.0 8.9 reduce-scatter.30
  258.7 10.1 reduce-scatter.32
  288.4 10.1 reduce-scatter.34
  403.7 10.4 reduce-scatter.36
  455.2 10.6 reduce-scatter.40
  486.8 65.9 reduce-scatter.66
  559.5 6.6 reduce-scatter.42
  598.0 8.1 reduce-scatter.44
  629.0 65.6 reduce-scatter.68
  701.5 6.7 reduce-scatter.46
  740.0 8.1 reduce-scatter.48
  770.7 65.5 reduce-scatter.70
  838.5 6.7 reduce-scatter.38
  847.3 8.9 reduce-scatter.50
  860.1 70.0 reduce-scatter.52
  933.9 68.0 reduce-scatter.58
  1006.2 63.2 reduce-scatter.54
  1073.9 63.0 reduce-scatter.56
  1140.9 116.9 reduce-scatter.60
  1261.9 117.0 reduce-scatter.62
  1383.0 117.0 reduce-scatter.64
where the time goes:
time: 1520 us; the launch traced here: 1510 us
  waiting for transfers between devices  707 us (47%)
  matrix products  261 us (17%)
  blocking collectives  256 us (17%)
  other arithmetic  148 us (10%)
  local copies, waits for them, and re-layouts  100 us (7%)
  starting transfers between devices  18.9 us (1%)
  between operations  17.5 us (1%)
    unnamed x25, waiting for transfers between devices  166 us
    reduce_scatter x1, waiting for transfers between devices, reduce_grads(): lax.psum_scatter(grad_set[6].astype(jnp.bfloat16), 'ctx', scatter_dimensi...  119 us
    reduce_scatter x1, waiting for transfers between devices, reduce_grads(): lax.psum_scatter(grad_set[7].astype(jnp.bfloat16), 'ctx', scatter_dimensi...  119 us
    reduce_scatter x1, waiting for transfers between devices, reduce_grads(): lax.psum_scatter(grad_set[8].astype(jnp.bfloat16), 'ctx', scatter_dimensi...  119 us
    all_gather x3, blocking collectives, on_device(): forward_keys_all = lax.all_gather(keys_own, 'ctx', axis=0, tiled=True)  103 us
    all_gather x3, blocking collectives, on_device(): forward_values_all = lax.all_gather(values_own, 'ctx', axis=0, tiled=True)  102 us
    dot_general x21, matrix products, dot_left_t(): lax.dot_general(left_op, right_op, (((0,), (0,)), ((), ())), preferred_el...  94.3 us
    reduce_scatter x1, waiting for transfers between devices, reduce_grads(): lax.psum_scatter(grad_set[3].astype(jnp.bfloat16), 'ctx', scatter_dimensi...  65.8 us
  transfers between devices with their start and end apart: 28, of which 19 were waited for; matrix products, arithmetic and copies ran while one was open for 18% of the time, Pallas kernels for 0%

commit v1 on v0

--- a/solution.py
+++ b/solution.py
@@ -1,6 +1,8 @@
 import jax
 import jax.numpy as jnp
 from jax import lax
+from jax.experimental import pallas as pl
+from jax.experimental.pallas import tpu as pltpu
 from jax.sharding import PartitionSpec as P
 
 HD = 96
@@ -107,7 +109,7 @@
     )
 
 
-def on_device(
+def on_device_wide(
     inputs, cotangent, norm_attn, w_query, w_key, w_value, w_out, norm_mlp, w_gate, w_up, w_down
 ):
     params = (
@@ -379,6 +381,1111 @@
     )
 
 
+MIB = 1 << 20
+CORE, SEQ, CTX, SECTION = range(4)
+LOG2E = 1.4426950408889634
+
+
+def in_hbm(array):
+    return pltpu.with_memory_space_constraint(array, pltpu.HBM)
+
+
+def in_vmem(array):
+    return pltpu.with_memory_space_constraint(array, pltpu.VMEM)
+
+
+HBM = pl.BlockSpec(memory_space=pltpu.HBM)
+VMEM = pl.BlockSpec(memory_space=pltpu.VMEM)
+SCALARS = pl.BlockSpec(memory_space=pltpu.SMEM)
+
+
+def whole_call(
+    body, outs, scratch=(), flops=0, nbytes=0, grant=16, in_specs=None, out_specs=None
+):
+    specs = {} if in_specs is None else {"in_specs": in_specs}
+    specs |= {} if out_specs is None else {"out_specs": out_specs}
+    return pl.pallas_call(
+        body,
+        out_shape=outs,
+        scratch_shapes=scratch,
+        compiler_params=pltpu.CompilerParams(vmem_limit_bytes=grant * MIB),
+        cost_estimate=pl.CostEstimate(flops=flops, bytes_accessed=nbytes, transcendentals=0),
+        **specs,
+    )
+
+
+def load_weights(weights):
+    count = len(weights)
+
+    def body(*refs):
+        copies = [
+            pltpu.make_async_copy(refs[at], refs[count + at], refs[-1].at[at])
+            for at in range(count)
+        ]
+        for copy in copies:
+            copy.start()
+        for copy in copies:
+            copy.wait()
+
+    return whole_call(
+        body,
+        tuple(pltpu.VMEM(weight.shape, weight.dtype) for weight in weights),
+        scratch=[pltpu.SemaphoreType.DMA((count,))],
+        nbytes=2 * sum(weight.size for weight in weights),
+        grant=4,
+        in_specs=[HBM] * count,
+        out_specs=(VMEM,) * count,
+    )(*map(in_hbm, weights))
+
+
+def own_half(rows, core, batches):
+    parts = rows.reshape(batches, 2, rows.shape[0] // batches // 2, rows.shape[1])
+    return jnp.where(core == 0, parts[:, 0], parts[:, 1])
+
+
+class Outbox:
+    def __init__(self, sems):
+        self.sems, self.copies = sems, []
+
+    def send(self, staged, target):
+        copy = pltpu.make_async_copy(staged, target, self.sems.at[len(self.copies)])
+        copy.start()
+        self.copies.append(copy)
+
+    def finish(self):
+        for copy in self.copies:
+            copy.wait()
+
+
+def rotate_head(head, cosine, sine_tab):
+    lower, upper = head[: HD // 2], head[HD // 2 :]
+    return jnp.concatenate(
+        [lower * cosine - upper * sine_tab, upper * cosine + lower * sine_tab], axis=0
+    )
+
+
+def rotate_back_head(head, cosine, sine_tab):
+    return rotate_head(head, cosine, -sine_tab)
+
+
+def project_heads(section_in, gain_vec, weights, cosine, sine_tab, indices):
+    rows, width = section_in.shape
+    batches = 2
+    span = rows // batches
+    groups = weights[1].shape[1] // HD
+    repeat = weights[0].shape[1] // HD // groups
+
+    def body(
+        at_ref, in_ref, gain_ref, query_ref, key_ref, value_ref, cos_ref, sin_ref,
+        mine_ref, theirs_ref, out_ref,
+    ):
+        cosine, sine_tab = cos_ref[...], sin_ref[...]
+        normed = normalize(in_ref[...].astype(jnp.float32), gain_ref[...])[0].astype(jnp.bfloat16)
+        mine_ref[...] = jnp.where(at_ref[SEQ] == 0, normed[:span], normed[span:])
+        theirs_ref[...] = jnp.where(at_ref[SEQ] == 0, normed[span:], normed[:span])
+        queries = dot_plain(normed, query_ref[...]).T
+        keys = dot_plain(normed, key_ref[...]).T
+        values = dot_plain(normed, value_ref[...]).T
+        for group in range(groups):
+            parts = [
+                rotate_head(queries[head * HD : (head + 1) * HD], cosine, sine_tab)
+                for head in range(group * repeat, (group + 1) * repeat)
+            ]
+            place = slice(group * HD, (group + 1) * HD)
+            parts += [rotate_head(keys[place], cosine, sine_tab), values[place]]
+            for at, part in enumerate(parts):
+                part = part.astype(jnp.bfloat16)
+                for seq in range(batches):
+                    lanes = slice(seq * span, (seq + 1) * span)
+                    out_ref[group * batches + seq, at * HD : (at + 1) * HD] = part[:, lanes]
+
+    columns = sum(weight.shape[1] for weight in weights)
+    return whole_call(
+        body,
+        (
+            pltpu.HBM((span, width), jnp.bfloat16),
+            pltpu.HBM((span, width), jnp.bfloat16),
+            pltpu.HBM((groups * batches, (repeat + 2) * HD, span), jnp.bfloat16),
+        ),
+        flops=2 * rows * width * columns,
+        nbytes=2 * width * columns,
+        in_specs=[SCALARS] + [VMEM] * 7,
+    )(indices, in_hbm(section_in), in_hbm(gain_vec[None]), *weights, cosine, sine_tab)
+
+
+def side_by_side(ref, first, last, blocks=None):
+    blocks = range(ref.shape[0]) if blocks is None else blocks
+    return jnp.concatenate([ref[block, first:last] for block in blocks], axis=1)
+
+
+def by_position(ref, first, last):
+    blocks, _, span = ref.shape
+    half = span // 2
+    lower = [ref[block, first:last, :half] for block in range(blocks)]
+    upper = [ref[block, first:last, half:] for block in reversed(range(blocks))]
+    return jnp.concatenate(lower + upper, axis=1)
+
+
+def to_blocks(ref, entries, rows, at):
+    blocks, _, span = ref.shape
+    half = span // 2
+    for first in range(0, rows.shape[1], half):
+        place = (at + first) // half
+        part = rows[:, first : first + half]
+        if place < blocks:
+            ref[place, entries, :half] = part
+        else:
+            ref[2 * blocks - 1 - place, entries, half:] = part
+
+
+TILE = 256
+
+
+def masked(scores, outside):
+    rows = scores.shape[0] - TILE
+    key_at = lax.broadcasted_iota(jnp.int32, (TILE, TILE), 0)
+    query_at = lax.broadcasted_iota(jnp.int32, (TILE, TILE), 1)
+    last = jnp.where(key_at <= query_at, scores[rows:], outside)
+    return last if rows == 0 else jnp.concatenate([scores[:rows], last], axis=0)
+
+
+def attend_heads(head_qkv, repeat):
+    blocks, _, span = head_qkv.shape
+    seq_len = blocks * span
+    scale = HD ** (-0.5) * LOG2E
+
+    def body(in_ref, out_ref, log_ref):
+        keys = by_position(in_ref, repeat * HD, (repeat + 1) * HD).T
+        values = by_position(in_ref, (repeat + 1) * HD, (repeat + 2) * HD)
+        for head in range(repeat):
+            entries = slice(head * HD, (head + 1) * HD)
+            queries = by_position(in_ref, entries.start, entries.stop)
+            for first in range(0, seq_len, TILE):
+                stop = first + TILE
+                scores = masked(dot_plain(keys[:stop], queries[:, first:stop]), -jnp.inf)
+                top_score = jnp.max(scores, axis=0, keepdims=True)
+                exp_scores = jnp.exp2((scores - top_score) * scale)
+                totals = jnp.sum(exp_scores, axis=0, keepdims=True)
+                prob_low = (exp_scores * (1.0 / totals)).astype(jnp.bfloat16)
+                mixed = dot_plain(values[:, :stop], prob_low).astype(jnp.bfloat16)
+                to_blocks(out_ref, entries, mixed, first)
+                log_ref[head, :, first:stop] = top_score * scale + jnp.log2(totals)
+
+    return whole_call(
+        body,
+        (
+            pltpu.HBM((blocks, repeat * HD, span), jnp.bfloat16),
+            pltpu.HBM((repeat, 1, seq_len), jnp.float32),
+        ),
+        flops=4 * repeat * seq_len * seq_len * HD,
+        nbytes=12 * seq_len * HD * repeat,
+    )(in_hbm(head_qkv))
+
+
+def attend_heads_back(head_qkv, head_grad, log_total, cosine, sine_tab, repeat):
+    blocks, _, span = head_qkv.shape
+    seq_len = blocks * span
+    scale = HD ** (-0.5)
+    key_place = slice(repeat * HD, (repeat + 1) * HD)
+    value_place = slice((repeat + 1) * HD, (repeat + 2) * HD)
+
+    def body(in_ref, grad_ref, log_ref, cos_ref, sin_ref, out_ref, key_acc, value_acc):
+        keys_t = by_position(in_ref, key_place.start, key_place.stop)
+        keys = keys_t.T
+        values = by_position(in_ref, value_place.start, value_place.stop).T
+        key_acc[...] = jnp.zeros_like(key_acc)
+        value_acc[...] = jnp.zeros_like(value_acc)
+        for head in range(repeat):
+            entries = slice(head * HD, (head + 1) * HD)
+            all_queries = by_position(in_ref, entries.start, entries.stop)
+            all_grads = by_position(grad_ref, entries.start, entries.stop)
+            for first in range(0, seq_len, TILE):
+                stop = first + TILE
+                place = slice(first, stop)
+                queries, grads = all_queries[:, place], all_grads[:, place]
+                scores = dot_plain(keys[:stop], queries) * (scale * LOG2E)
+                prob = jnp.exp2(masked(scores - log_ref[head, :, place], -jnp.inf))
+                prob_grad = dot_plain(values[:stop], grads)
+                inner_sum = jnp.sum(prob * prob_grad, axis=0, keepdims=True)
+                score_grad = (prob * (prob_grad - inner_sum)).astype(jnp.bfloat16)
+                prob_low = prob.astype(jnp.bfloat16)
+                query_grad = rotate_back_head(
+                    dot_plain(keys_t[:, :stop], score_grad) * scale,
+                    cos_ref[:, place],
+                    sin_ref[:, place],
+                ).astype(jnp.bfloat16)
+                to_blocks(out_ref, entries, query_grad, first)
+                key_acc[:, :stop] += dot_right_t(queries, score_grad)
+                value_acc[:, :stop] += dot_right_t(grads, prob_low)
+        key_grad = rotate_back_head(key_acc[...] * scale, cos_ref[...], sin_ref[...])
+        to_blocks(out_ref, key_place, key_grad.astype(jnp.bfloat16), 0)
+        to_blocks(out_ref, value_place, value_acc[...].astype(jnp.bfloat16), 0)
+
+    return whole_call(
+        body,
+        pltpu.HBM(head_qkv.shape, jnp.bfloat16),
+        scratch=[pltpu.VMEM((HD, seq_len), jnp.float32)] * 2,
+        flops=10 * repeat * seq_len * seq_len * HD,
+        nbytes=16 * repeat * seq_len * HD,
+    )(in_hbm(head_qkv), head_grad, *map(in_hbm, (log_total, cosine, sine_tab)))
+
+
+def rows_side_by_side(ref, first, last, batches):
+    groups = ref.shape[0] // batches
+    return jnp.concatenate(
+        [
+            side_by_side(
+                ref, first, last, [group * batches + seq for seq in range(batches)]
+            )
+            for group in range(groups)
+        ],
+        axis=0,
+    )
+
+
+def project_out(arrived, out_w, batches):
+    _, depth, span = arrived.shape
+    width, heads = out_w.shape
+    rows = batches * span
+
+    def body(in_ref, weight_ref, mixed_ref, out_ref):
+        mixed = rows_side_by_side(in_ref, 0, depth, batches)
+        mixed_ref[...] = mixed.T
+        out_ref[...] = dot_plain(weight_ref[...], mixed).T.astype(jnp.bfloat16)
+
+    return whole_call(
+        body,
+        (
+            pltpu.HBM((rows, heads), jnp.bfloat16),
+            pltpu.HBM((rows, width), jnp.bfloat16),
+        ),
+        flops=2 * rows * width * heads,
+        nbytes=2 * width * heads,
+    )(arrived, out_w)
+
+
+def full_block(array):
+    return pl.BlockSpec(
+        array.shape, lambda *_: (0,) * len(array.shape), pipeline_mode=pl.Buffered(1)
+    )
+
+
+def stepped_call(
+    body, indices, grid, in_specs, outs, out_specs, scratch, flops, nbytes, grant, aliases=None
+):
+    call = pl.pallas_call(
+        body,
+        grid_spec=pltpu.PrefetchScalarGridSpec(
+            num_scalar_prefetch=1,
+            grid=grid,
+            in_specs=in_specs,
+            out_specs=out_specs,
+            scratch_shapes=scratch,
+        ),
+        out_shape=outs,
+        input_output_aliases=aliases or {},
+        compiler_params=pltpu.CompilerParams(
+            dimension_semantics=("arbitrary",) * len(grid), vmem_limit_bytes=grant * MIB
+        ),
+        cost_estimate=pl.CostEstimate(flops=flops, bytes_accessed=nbytes, transcendentals=0),
+    )
+    return lambda *arrays: call(indices, *arrays)
+
+
+def weight_slots(count, width):
+    return [
+        pltpu.VMEM((2, count, width, HIDDEN), jnp.bfloat16),
+        pltpu.SemaphoreType.DMA((2, count)),
+    ]
+
+
+class Stream:
+    def __init__(self, weights, slots, sems, steps, first=0):
+        self.weights, self.slots, self.sems, self.first = weights, slots, sems, first
+        self.step, self.begins = pl.program_id(0), pl.program_id(1) == 0
+
+        @pl.when(self.begins & (self.step == 0))
+        def _():
+            for copy in self.copies(0):
+                copy.start()
+
+        @pl.when(self.begins & (self.step + 1 < steps))
+        def _():
+            for copy in self.copies(self.step + 1):
+                copy.start()
+
+    def copies(self, step):
+        slot = step % 2
+        first = pl.multiple_of((self.first + step) * HIDDEN, HIDDEN)
+        place = pl.ds(first, HIDDEN)
+        return [
+            pltpu.make_async_copy(
+                weight.at[:, place], self.slots.at[slot, at], self.sems.at[slot, at]
+            )
+            for at, weight in enumerate(self.weights)
+        ]
+
+    def blocks(self):
+        @pl.when(self.begins)
+        def _():
+            for copy in self.copies(self.step):
+                copy.wait()
+
+        return [self.slots[self.step % 2, at] for at in range(len(self.weights))]
+
+
+def hidden_factors(gate_pre, up_pre):
+    sigmoid_g = 0.5 + 0.5 * jnp.tanh(0.5 * gate_pre)
+    silu_gate = gate_pre * sigmoid_g
+    return silu_gate * up_pre, up_pre * (sigmoid_g + silu_gate * (1.0 - sigmoid_g)), silu_gate
+
+
+HIDDEN = 512
+
+
+class Blocks:
+    def __init__(self, weights, held, sems):
+        self.held = held
+        hidden = weights[0].shape[1]
+        self.places = [slice(first, first + HIDDEN) for first in range(0, hidden, HIDDEN)]
+        self.copies = [
+            [
+                pltpu.make_async_copy(
+                    weight.at[:, place], held.at[at, step], sems.at[at, step]
+                )
+                for at, weight in enumerate(weights)
+            ]
+            for step, place in enumerate(self.places)
+        ]
+        self.start(0)
+
+    def start(self, step):
+        for copy in self.copies[step]:
+            copy.start()
+
+    def get(self, step, at):
+        self.copies[step][at].wait()
+        return self.held[at, step]
+
+
+def block_scratch(weights):
+    width, hidden = weights[0].shape
+    count, steps = len(weights), hidden // HIDDEN
+    return [
+        pltpu.VMEM((count, steps, width, HIDDEN), jnp.bfloat16),
+        pltpu.SemaphoreType.DMA((count, steps)),
+    ]
+
+
+def feed_forward(section_in, attn_own, attn_other, gain_vec, weights, batches, indices):
+    rows, width = section_in.shape
+    hidden = weights[0].shape[1]
+    half = (batches, rows // batches // 2, width)
+
+    def body(
+        at_ref, in_ref, own_ref, other_ref, gain_ref, gate_ref, up_ref, down_ref,
+        mid_out, low_out, gate_f_out, up_f_out, keep_out, send_out,
+        mid_ref, low_ref, gate_f_ref, up_f_ref, keep_ref, send_ref, sems, held, block_sems,
+    ):
+        blocks = Blocks((gate_ref, up_ref, down_ref), held, block_sems)
+        for step in range(1, len(blocks.places)):
+            blocks.start(step)
+        outbox = Outbox(sems)
+        middle = in_ref[...].astype(jnp.float32) + (
+            own_ref[...].astype(jnp.float32) + other_ref[...].astype(jnp.float32)
+        )
+        mid_ref[...] = middle
+        outbox.send(mid_ref, mid_out)
+        low = normalize(middle, gain_ref[...])[0].astype(jnp.bfloat16)
+        low_ref[...] = own_half(low, at_ref[CORE], batches)
+        outbox.send(low_ref, low_out)
+        total = None
+        for step, place in enumerate(blocks.places):
+            inner, gate_f, up_f = hidden_factors(
+                dot_plain(low, blocks.get(step, 0)), dot_plain(low, blocks.get(step, 1))
+            )
+            gate_f_ref[:, place] = gate_f.astype(jnp.bfloat16)
+            up_f_ref[:, place] = up_f.astype(jnp.bfloat16)
+            part = dot_right_t(inner.astype(jnp.bfloat16), blocks.get(step, 2))
+            total = part if total is None else total + part
+        outbox.send(gate_f_ref, gate_f_out)
+        outbox.send(up_f_ref, up_f_out)
+        total = total.astype(jnp.bfloat16)
+        keep_ref[...] = own_half(total, at_ref[CORE], batches)
+        send_ref[...] = own_half(total, 1 - at_ref[CORE], batches)
+        outbox.send(send_ref, send_out)
+        outbox.send(keep_ref, keep_out)
+        outbox.finish()
+
+    shapes = [
+        ((rows, width), jnp.float32),
+        (half, jnp.bfloat16),
+        ((rows, hidden), jnp.bfloat16),
+        ((rows, hidden), jnp.bfloat16),
+        (half, jnp.bfloat16),
+        (half, jnp.bfloat16),
+    ]
+    return whole_call(
+        body,
+        tuple(pltpu.HBM(*shape) for shape in shapes),
+        scratch=[pltpu.VMEM(*shape) for shape in shapes]
+        + [pltpu.SemaphoreType.DMA((len(shapes),))]
+        + block_scratch(weights),
+        flops=6 * rows * width * hidden,
+        nbytes=6 * width * hidden,
+        grant=36,
+        in_specs=[SCALARS] + [VMEM] * 4 + [HBM] * 3,
+        out_specs=(HBM,) * len(shapes),
+    )(
+        indices, in_hbm(section_in), in_hbm(attn_own), attn_other, in_hbm(gain_vec[None]),
+        *map(in_hbm, weights),
+    )
+
+
+def feed_forward_back(upstream, gate_f, up_f, weights):
+    rows, width = upstream.shape
+    hidden = weights[0].shape[1]
+
+    def body(
+        upstream_ref, gate_f_ref, up_f_ref, down_ref, gate_ref, up_ref, out_ref, held, block_sems
+    ):
+        blocks = Blocks((down_ref, gate_ref, up_ref), held, block_sems)
+        for step in range(1, len(blocks.places)):
+            blocks.start(step)
+        low = upstream_ref[...]
+        total = None
+        for step, place in enumerate(blocks.places):
+            inner_grad = dot_plain(low, blocks.get(step, 0))
+            gate_grad = (inner_grad * gate_f_ref[:, place].astype(jnp.float32)).astype(jnp.bfloat16)
+            up_grad = (inner_grad * up_f_ref[:, place].astype(jnp.float32)).astype(jnp.bfloat16)
+            part = dot_right_t(gate_grad, blocks.get(step, 1))
+            part += dot_right_t(up_grad, blocks.get(step, 2))
+            total = part if total is None else total + part
+        out_ref[...] = total.astype(jnp.bfloat16)
+
+    return whole_call(
+        body,
+        pltpu.HBM((rows, width), jnp.bfloat16),
+        scratch=block_scratch(weights),
+        flops=6 * rows * width * hidden,
+        nbytes=6 * width * hidden,
+        grant=34,
+        in_specs=[VMEM] * 3 + [HBM] * 3,
+    )(*map(in_hbm, (upstream, gate_f, up_f, weights[2], *weights[:2])))
+
+
+def middle_back(
+    upstream, part_own, part_other, middle, gain_vec, out_w, groups, batches, indices
+):
+    rows, width = middle.shape
+    span = rows // batches
+    depth = out_w.shape[1] // groups
+
+    def body(
+        at_ref, up_ref, own_ref, other_ref, mid_ref, gain_ref, weight_ref, grad_out, low_out, head_out,
+        grad_ref, low_ref, head_ref, sems,
+    ):
+        outbox = Outbox(sems)
+        normed_grad = own_ref[...].astype(jnp.float32) + other_ref[...].astype(jnp.float32)
+        _, normed, inv_scale = normalize(mid_ref[...], gain_ref[...])
+        down_grad = norm_back(normed_grad, normed, inv_scale, gain_ref[...])[0]
+        middle_grad = up_ref[...].astype(jnp.float32) + down_grad
+        grad_ref[...] = own_half(middle_grad, at_ref[CORE], batches)
+        outbox.send(grad_ref, grad_out)
+        low = middle_grad.astype(jnp.bfloat16)
+        low_ref[...] = low
+        outbox.send(low_ref, low_out)
+        heads = dot_plain(low, weight_ref[...]).T.astype(jnp.bfloat16)
+        for group in range(groups):
+            for seq in range(batches):
+                head_ref[group * batches + seq] = heads[
+                    group * depth : (group + 1) * depth, seq * span : (seq + 1) * span
+                ]
+        outbox.send(head_ref, head_out)
+        outbox.finish()
+
+    shapes = [
+        ((batches, span // 2, width), jnp.float32),
+        ((rows, width), jnp.bfloat16),
+        ((groups * batches, depth, span), jnp.bfloat16),
+    ]
+    return whole_call(
+        body,
+        tuple(pltpu.HBM(*shape) for shape in shapes),
+        scratch=[pltpu.VMEM(*shape) for shape in shapes] + [pltpu.SemaphoreType.DMA((3,))],
+        flops=2 * rows * width * groups * depth,
+        nbytes=2 * width * groups * depth,
+        in_specs=[SCALARS] + [VMEM] * 6,
+        out_specs=(HBM,) * 3,
+    )(
+        indices, in_hbm(upstream), in_hbm(part_own), part_other, in_hbm(middle), in_hbm(gain_vec[None]),
+        out_w,
+    )
+
+
+def heads_back(row_grads, weights, batches, indices, depth):
+    span = row_grads.shape[2]
+    rows = batches * span
+    width = weights[0].shape[0]
+    first = depth - 2 * HD
+
+    def body(at_ref, grad_ref, query_ref, key_ref, value_ref, keep_ref, send_ref):
+        def picked(start, stop):
+            return rows_side_by_side(grad_ref, start, stop, batches)
+
+        total = dot_plain(query_ref[...], picked(0, first))
+        total += dot_plain(key_ref[...], picked(first, first + HD))
+        total += dot_plain(value_ref[...], picked(first + HD, depth))
+        total = total.T.astype(jnp.bfloat16)
+        keep_ref[...] = own_half(total, at_ref[CORE], batches)
+        send_ref[...] = own_half(total, 1 - at_ref[CORE], batches)
+
+    columns = sum(weight.shape[1] for weight in weights)
+    return whole_call(
+        body,
+        (pltpu.HBM((batches, span // 2, width), jnp.bfloat16),) * 2,
+        flops=2 * rows * width * columns,
+        nbytes=2 * width * columns,
+        in_specs=[SCALARS] + [VMEM] * 4,
+    )(indices, row_grads, *weights)
+
+
+def input_back(
+    part_own, part_other, middle_grad, section_in, gain_vec, indices, other, last=None
+):
+    batches, half_rows, width = middle_grad.shape
+
+    def body(at_ref, own_ref, other_ref, grad_ref, in_ref, gain_ref, *refs):
+        rows = own_half(in_ref[...], at_ref[CORE], batches).astype(jnp.float32)
+        normed_grad = own_ref[...].astype(jnp.float32) + other_ref[...].astype(jnp.float32)
+        _, normed, inv_scale = normalize(rows, gain_ref[...])
+        down_grad = norm_back(normed_grad, normed, inv_scale, gain_ref[...])[0]
+        total = grad_ref[...] + down_grad
+        if last is None:
+            given_ref, out_ref, low_ref = refs
+            low = total.astype(jnp.bfloat16)
+            low_ref[...] = jnp.where(at_ref[SECTION] == 0, given_ref[...], low)
+        else:
+            given_ref, last_ref, out_ref, cast_ref = refs
+            total = jnp.where(at_ref[SECTION] == 0, total, given_ref[...])
+            cast_ref[...] = last_ref[...].astype(jnp.float32)
+        out_ref[...] = total
+
+    shape = (batches, half_rows, width)
+    outs = [pltpu.HBM(shape, jnp.float32), pltpu.HBM(shape, jnp.bfloat16)]
+    if last is not None:
+        outs[1] = pltpu.HBM(last.shape, jnp.float32)
+    more = () if last is None else (in_hbm(last),)
+    return whole_call(
+        body,
+        tuple(outs),
+        nbytes=24 * batches * half_rows * width,
+        in_specs=[SCALARS] + [VMEM] * (6 + len(more)),
+    )(
+        indices, in_hbm(part_own), part_other, in_hbm(middle_grad), in_hbm(section_in),
+        in_hbm(gain_vec[None]), in_hbm(other), *more,
+    )
+
+
+ROWS = 1024
+
+
+class Rows:
+    def __init__(self, source, target, sems):
+        self.target = target
+        self.first, self.at = pl.program_id(0) == 0, pl.program_id(1)
+        self.copies = [
+            pltpu.make_async_copy(
+                source.at[pl.ds(first, ROWS)], target.at[pl.ds(first, ROWS)], sems.at[at]
+            )
+            for at, first in enumerate(range(0, target.shape[0], ROWS))
+        ]
+
+        @pl.when(self.first & (self.at == 0))
+        def _():
+            for copy in self.copies:
+                copy.start()
+
+        for at, copy in enumerate(self.copies):
+
+            @pl.when(self.first & (self.at == at))
+            def _():
+                copy.wait()
+
+        self.place = pl.ds(pl.multiple_of(self.at * ROWS, ROWS), ROWS)
+
+    def chunk(self):
+        return self.target[self.place]
+
+    def columns(self, ctx_at, owned):
+        first = pl.multiple_of((ctx_at // 2) * 2 * owned, 2 * owned)
+        pair = self.target[self.place, pl.ds(first, 2 * owned)].T
+        return jnp.where(ctx_at % 2 == 0, pair[:owned], pair[owned:])
+
+
+def row_scratch(rows, width):
+    return [pltpu.VMEM((rows, width), jnp.bfloat16), pltpu.SemaphoreType.DMA((rows // ROWS,))]
+
+
+def hidden_of_all(mlp_all, gate_w, up_w, first, steps, indices, blocks, kept=()):
+    rows, width = mlp_all.shape
+    hidden = gate_w.shape[1]
+    owned = width // blocks
+    first_part = not kept
+
+    def body(at_ref, all_ref, gate_ref, up_ref, *refs):
+        target, row_sems, slots, sems = refs[-4:]
+        inner_ref, gate_f_ref, up_f_ref, *cols_ref = refs[len(kept) : -4]
+        stream = Stream((gate_ref, up_ref), slots, sems, steps, first)
+        fetched = Rows(all_ref, target, row_sems)
+        gate_block, up_block = stream.blocks()
+        low = fetched.chunk()
+        inner, gate_f, up_f = hidden_factors(dot_plain(low, gate_block), dot_plain(low, up_block))
+        inner_ref[...] = inner.astype(jnp.bfloat16)
+        gate_f_ref[...] = gate_f.astype(jnp.bfloat16)
+        up_f_ref[...] = up_f.astype(jnp.bfloat16)
+        if first_part:
+
+            @pl.when(stream.step == 0)
+            def _():
+                cols_ref[0][:, fetched.place] = fetched.columns(at_ref[CTX], owned)
+
+    cols = pltpu.HBM((owned, rows), jnp.bfloat16)
+    block = pl.BlockSpec((ROWS, HIDDEN), lambda step, at, *_: (at, first + step))
+    return stepped_call(
+        body,
+        indices,
+        (steps, rows // ROWS),
+        [HBM] * (3 + len(kept)),
+        (pltpu.HBM((rows, hidden), jnp.bfloat16),) * 3 + (cols,) * first_part,
+        (block,) * 3 + (full_block(cols),) * first_part,
+        row_scratch(rows, width) + weight_slots(2, width),
+        4 * rows * width * HIDDEN * steps,
+        2 * rows * width + (4 * width + 6 * rows) * HIDDEN * steps,
+        40,
+        aliases={4 + i: i for i in range(len(kept))},
+    )(*map(in_hbm, (mlp_all, gate_w, up_w, *kept)))
+
+
+def hidden_grads(upstream_rows, down_w, hidden_kept, indices, weights, first, steps, kept=()):
+    rows, width = upstream_rows.shape
+    hidden = down_w.shape[1]
+    owned = hidden_kept[3].shape[0]
+    chunks = rows // ROWS
+
+    def body(
+        at_ref, rows_ref, down_ref, inner_ref, gate_f_ref, up_f_ref, mlp_ref, gate_ref, up_ref, *refs
+    ):
+        *outs, cols_ref, target, row_sems, slots, sems = refs[len(kept) :]
+        stream = Stream((down_ref,), slots, sems, steps, first)
+        fetched = Rows(rows_ref, target, row_sems)
+        (down_block,) = stream.blocks()
+
+        @pl.when(stream.step == 0)
+        def _():
+            cols_ref[:, fetched.place] = fetched.columns(at_ref[CTX], owned)
+
+        inner_grad = dot_plain(fetched.chunk(), down_block)
+        gate_grad = (inner_grad * gate_f_ref[...].astype(jnp.float32)).astype(jnp.bfloat16)
+        up_grad = (inner_grad * up_f_ref[...].astype(jnp.float32)).astype(jnp.bfloat16)
+        mlp_cols = mlp_ref[:, fetched.place]
+        pieces = (
+            dot_plain(mlp_cols, gate_grad),
+            dot_plain(mlp_cols, up_grad),
+            dot_plain(cols_ref[:, fetched.place], inner_ref[...]),
+        )
+
+        @pl.when(stream.begins)
+        def _():
+            for out, piece in zip(outs, pieces):
+                out[...] = piece
+
+        @pl.when(jnp.logical_not(stream.begins))
+        def _():
+            for out, piece in zip(outs, pieces):
+                out[...] += piece
+
+        @pl.when(fetched.at == chunks - 1)
+        def _():
+            products = outs[0][...] * gate_ref[...].astype(jnp.float32)
+            products += outs[1][...] * up_ref[...].astype(jnp.float32)
+            products = jnp.sum(products, axis=1, keepdims=True)
+            outs[3][...] = jnp.where(stream.step == 0, products, outs[3][...] + products)
+
+    owned_block = pl.BlockSpec((owned, HIDDEN), lambda step, at, at_ref: (at_ref[CTX], first + step))
+    out_block = pl.BlockSpec((owned, HIDDEN), lambda step, at, *_: (0, first + step))
+    row_block = pl.BlockSpec((ROWS, HIDDEN), lambda step, at, *_: (at, first + step))
+    sums = pltpu.HBM((owned, 1), jnp.float32)
+    return stepped_call(
+        body,
+        indices,
+        (steps, chunks),
+        [HBM] * 2
+        + [row_block] * 3
+        + [full_block(hidden_kept[3])]
+        + [owned_block] * 2
+        + [HBM] * len(kept),
+        (pltpu.HBM((owned, hidden), jnp.float32),) * 3 + (sums,),
+        (out_block,) * 3 + (full_block(sums),),
+        [pltpu.VMEM((owned, rows), jnp.bfloat16)] + row_scratch(rows, width) + weight_slots(1, width),
+        (2 * rows * width + 6 * owned * rows) * HIDDEN * steps,
+        2 * rows * width + (2 * width + 6 * rows) * HIDDEN * steps,
+        40,
+        aliases={9 + i: i for i in range(len(kept))},
+    )(*map(in_hbm, (upstream_rows, down_w, *hidden_kept, *weights, *kept)))
+
+
+def taken(place, groups, targets, sems):
+    for at, (sources, target) in enumerate(zip(groups, targets)):
+        for number, source in enumerate(sources):
+
+            @pl.when(place == number)
+            def _():
+                pltpu.make_async_copy(source, target, sems.at[at]).start()
+
+    for at, (sources, target) in enumerate(zip(groups, targets)):
+        pltpu.make_async_copy(sources[0], target, sems.at[at]).wait()
+
+
+def split_owners(total, owned, seq_at, keep_ref, send_ref):
+    pairs = keep_ref.shape[0]
+    for pair in range(pairs):
+        lower, upper = (total(2 * pair * owned + half * owned, owned) for half in range(2))
+        keep_ref[pair] = jnp.where(seq_at == 0, lower, upper)
+        send_ref[pair] = jnp.where(seq_at == 0, upper, lower)
+
+
+def head_weight_grads(head_grads, attn_rows, indices):
+    blocks, depth, span = head_grads[0].shape
+    rows, width = attn_rows[0].shape
+    owned = width // blocks
+
+    def body(
+        at_ref, grad_0, grad_1, rows_0, rows_1, out_ref, grad_ref, rows_ref, sems
+    ):
+        groups = ((grad_0, grad_1), (rows_0, rows_1))
+        taken(at_ref[SECTION], groups, (grad_ref, rows_ref), sems)
+        total = dot_plain(side_by_side(grad_ref, 0, depth), rows_ref[...]).T.astype(jnp.bfloat16)
+        for owner in range(blocks):
+            out_ref[owner, :depth] = grad_ref[owner]
+            own = slice(owner * owned, (owner + 1) * owned)
+            for at in range(depth // span):
+                place = slice(depth + at * owned, depth + (at + 1) * owned)
+                out_ref[owner, place] = total[own, at * span : (at + 1) * span]
+
+    return whole_call(
+        body,
+        pltpu.HBM((blocks, depth + depth // span * owned, span), jnp.bfloat16),
+        scratch=[
+            pltpu.VMEM(head_grads[0].shape, jnp.bfloat16),
+            pltpu.VMEM((rows, width), jnp.bfloat16),
+            pltpu.SemaphoreType.DMA((2,)),
+        ],
+        flops=2 * rows * width * depth,
+        nbytes=2 * rows * width,
+        in_specs=[SCALARS] + [HBM] * 4,
+    )(indices, *map(in_hbm, (*head_grads, *attn_rows)))
+
+
+def out_weight_grads(middle_lows, mixed, indices, blocks):
+    rows, width = middle_lows[0].shape
+    heads = mixed[0].shape[1]
+    owned = width // blocks
+
+    def body(
+        at_ref, low_0, low_1, mixed_0, mixed_1, keep_ref, send_ref, low_ref, mixed_ref, sems
+    ):
+        groups = ((low_0, low_1), (mixed_0, mixed_1))
+        taken(at_ref[SECTION], groups, (low_ref, mixed_ref), sems)
+        total = dot_plain(low_ref[...].T, mixed_ref[...]).astype(jnp.bfloat16)
+        split_owners(
+            lambda first, size: total[first : first + size], owned, at_ref[SEQ], keep_ref, send_ref
+        )
+
+    half = pltpu.HBM((blocks // 2, owned, heads), jnp.bfloat16)
+    return whole_call(
+        body,
+        (half, half),
+        scratch=[
+            pltpu.VMEM((rows, width), jnp.bfloat16),
+            pltpu.VMEM((rows, heads), jnp.bfloat16),
+            pltpu.SemaphoreType.DMA((2,)),
+        ],
+        flops=2 * rows * width * heads,
+        nbytes=2 * width * heads,
+        grant=18,
+        in_specs=[SCALARS] + [HBM] * 4,
+    )(indices, *map(in_hbm, (*middle_lows, *mixed)))
+
+
+def own_weight_grads(arrived, weights, more_sums, indices, depth):
+    blocks, size, span = arrived.shape
+    owned = (size - depth) * span // depth
+    batches = 2
+    first = depth - 2 * HD
+
+    def body(
+        _, in_ref, query_ref, key_ref, value_ref, first_ref, second_ref,
+        query_out, key_out, value_out, sum_out,
+    ):
+        totals = [
+            sum(
+                jnp.concatenate(
+                    [
+                        in_ref[block + seq, depth + at * owned : depth + (at + 1) * owned]
+                        for at in range(depth // span)
+                    ],
+                    axis=1,
+                ).astype(jnp.float32)
+                for seq in range(batches)
+            )
+            for block in range(0, blocks, batches)
+        ]
+        products = 0.0
+        for ref, out, start, stop in (
+            (query_ref, query_out, 0, first),
+            (key_ref, key_out, first, first + HD),
+            (value_ref, value_out, first + HD, depth),
+        ):
+            grad = jnp.concatenate([total[:, start:stop] for total in totals], axis=1)
+            out[...] = grad
+            products += jnp.sum(grad * ref[...].astype(jnp.float32), axis=1, keepdims=True)
+        sums = (products, first_ref[...] + second_ref[...])
+        for row, column in enumerate(sums):
+            sum_out[row : row + 1] = jnp.broadcast_to(column, (owned, 128)).T[:1]
+
+    outs = [pltpu.HBM((owned, weight.shape[1]), jnp.float32) for weight in weights]
+    outs.append(pltpu.HBM((2, owned), jnp.float32))
+    return stepped_call(
+        body,
+        indices,
+        (1,),
+        [full_block(arrived)]
+        + [
+            pl.BlockSpec((owned, weight.shape[1]), lambda step, at_ref: (at_ref[CTX], 0))
+            for weight in weights
+        ]
+        + [full_block(more_sums[0])] * 2,
+        outs,
+        [full_block(out) for out in outs],
+        [],
+        0,
+        6 * blocks * depth * owned,
+        18,
+    )(arrived, *map(in_hbm, weights), *more_sums)
+
+
+def swap_blocks(pieces, members=None):
+    return lax.all_to_all(
+        pieces, "ctx", split_axis=0, concat_axis=0, axis_index_groups=members
+    )
+
+
+def other_core(array):
+    return lax.ppermute(array, "tp", [(0, 1), (1, 0)])
+
+
+def tied(*arrays):
+    return lax.optimization_barrier(arrays)
+
+
+def on_device(
+    inputs, cotangent, norm_attn, w_query, w_key, w_value, w_out, norm_mlp, w_gate, w_up, w_down
+):
+    params = tuple(
+        weight[0]
+        for weight in (norm_attn, w_query, w_key, w_value, w_out, norm_mlp, w_gate, w_up, w_down)
+    )
+    gain_attn, query_w, key_w, value_w, out_w, gain_mlp, gate_w, up_w, down_w = params
+    batches, local_rows, width = inputs.shape
+    span_rows = local_rows * lax.axis_size("tp")
+    blocks = lax.axis_size("ctx")
+    seq_len = span_rows * blocks
+    half_rows = span_rows // 2
+    halves = 2 * blocks
+    groups = key_w.shape[1] // HD
+    repeat = query_w.shape[1] // key_w.shape[1]
+    section_at = lax.axis_index("pipe")
+    sections = lax.axis_size("pipe")
+    ctx_at = lax.axis_index("ctx")
+    tp_at = lax.axis_index("tp")
+    seq_at = ctx_at % batches
+    rows = batches * span_rows
+    owned = width // blocks
+    indices = jnp.stack([tp_at, seq_at, ctx_at, section_at])
+    own_pos = place_rows(
+        ctx_at * span_rows + jnp.arange(span_rows, dtype=jnp.int32), half_rows, halves
+    )
+    cosine, sine_tab = (
+        jnp.tile(tab[:, : HD // 2].T, (1, batches)) for tab in rotary_tables(own_pos)
+    )
+    all_cosine, all_sine = (tab[:, : HD // 2].T for tab in rotary_tables(jnp.arange(seq_len)))
+    neighbours = [(i, i ^ 1) for i in range(blocks)]
+    same_x = [list(range(x, blocks, 2)) for x in range(2)]
+
+    def tp_rows(part):
+        return lax.all_gather(part, "tp", axis=1, tiled=True).reshape(rows, width)
+
+    def own_part(full):
+        full = full.reshape(batches, span_rows, width)
+        return lax.dynamic_slice_in_dim(full, tp_at * local_rows, local_rows, 1)
+
+    def here(per_section):
+        picked = per_section[0]
+        for section, value in enumerate(per_section[1:], 1):
+            picked = jnp.where(section_at == section, value, picked)
+        return picked
+
+    def rows_of_all(part):
+        return lax.all_gather(part.reshape(-1, width), ("ctx", "tp"), axis=0, tiled=True)
+
+    def part_of_sequence(mine, theirs):
+        pairs = [(2 * i + i % 2, 2 * (i ^ 1) + i % 2) for i in range(blocks)]
+        theirs = lax.ppermute(theirs, ("ctx", "tp"), pairs)
+        return jnp.where(tp_at == seq_at, mine, theirs)
+
+    def rows_of_sequence(part):
+        members = [
+            [2 * (pair * batches + seq) + core for pair in range(groups) for core in range(2)]
+            for seq in range(batches)
+        ]
+        return lax.all_gather(
+            part, ("ctx", "tp"), axis=0, tiled=True, axis_index_groups=members
+        )
+
+    def added(keep, send):
+        arrived = lax.ppermute(send, "ctx", neighbours)
+        return (keep.astype(jnp.float32) + arrived.astype(jnp.float32)).astype(jnp.bfloat16)
+
+    def owned_gain(gain_vec):
+        return lax.dynamic_slice_in_dim(gain_vec, ctx_at * owned, owned, 0)
+
+    states, attn_rows, mlp_parts = [], [], []
+    arrived = inputs
+    weights = (key_w, value_w, out_w)
+    hidden_weights = (gate_w, up_w, down_w)
+    held = tuple(map(in_hbm, weights))
+    for section in range(sections):
+        section_in = tp_rows(arrived)
+        mine, theirs, pieces = project_heads(
+            section_in, gain_attn, (in_hbm(query_w), *held[:2]), cosine, sine_tab, indices
+        )
+        attn_part = part_of_sequence(mine, theirs)
+        head_qkv, attn_part = tied(swap_blocks(pieces), attn_part)
+        if section == 0:
+            cotangent_rows, *loaded = tied(cotangent, mine, *weights)
+            cotangent_rows = tp_rows(cotangent_rows)
+            held = tuple(map(in_vmem, load_weights(loaded[1:])))
+            head_qkv, cotangent_rows = tied(head_qkv, cotangent_rows)
+        head_mixed, log_total = attend_heads(head_qkv, repeat)
+        if section == 1:
+            head_mixed, attn_rows[0] = tied(head_mixed, attn_rows[0])
+        mixed, attn_own = project_out(swap_blocks(head_mixed), held[2], batches)
+        if section == 0:
+            attn_own, attn_part = tied(attn_own, attn_part)
+            attn_rows.append(rows_of_sequence(attn_part))
+        middle, mlp_part, gate_f, up_f, part_own, part_sent = feed_forward(
+            section_in, attn_own, other_core(attn_own), gain_mlp, hidden_weights, batches, indices
+        )
+        mlp_parts.append(mlp_part)
+        if section == 1:
+            mlp_part, part_sent = tied(here(mlp_parts), part_sent)
+            mlp_rows = rows_of_all(mlp_part)
+        total = part_own.astype(jnp.float32) + other_core(part_sent).astype(jnp.float32)
+        outgoing = (own_part(middle) + total).astype(jnp.bfloat16)
+        states.append((section_in, head_qkv, log_total, mixed, middle, gate_f, up_f, outgoing))
+        if section == 0:
+            arrived = shifted(outgoing, "pipe", 1)
+    section_out = here([state[-1] for state in states])
+
+    def recompute(first, steps, after, kept=()):
+        later_rows, _ = tied(mlp_rows, after)
+        return hidden_of_all(later_rows, gate_w, up_w, first, steps, indices, blocks, kept)
+
+    all_steps = gate_w.shape[1] // HIDDEN
+    depth = (repeat + 2) * HD
+    middle_lows, head_parts = [None] * 2, [None] * 2
+    for section in (1, 0):
+        section_in, head_qkv, log_total, mixed, middle, gate_f, up_f, _ = states[section]
+        upstream = cotangent_rows if section == 1 else tp_rows(arrived)
+        if section == 0:
+            upstream, arrived = tied(upstream, arrived)
+            upstream_rows = rows_of_all(arrived)
+        part_own = feed_forward_back(upstream, gate_f, up_f, hidden_weights)
+        middle_grad, middle_lows[section], mixed_grad = middle_back(
+            upstream, part_own, other_core(part_own), middle, gain_mlp, held[2], groups, batches,
+            indices,
+        )
+        head_grad = swap_blocks(mixed_grad)
+        if section == 0:
+            hidden_kept = recompute(1, all_steps - 2, mixed_grad, hidden_kept)
+            head_grad, *hidden_kept = tied(head_grad, *hidden_kept)
+        head_parts[section] = head_grads = attend_heads_back(
+            head_qkv, head_grad, log_total, all_cosine, all_sine, repeat
+        )
+        if section == 1:
+            row_grads, section_out = tied(swap_blocks(head_grads), section_out)
+            attn_part, _ = tied(attn_part, head_grads)
+            attn_rows.append(rows_of_sequence(attn_part))
+        else:
+            pieces = head_weight_grads(head_parts, attn_rows, indices)
+            row_grads = swap_blocks(pieces)
+            middle_lows[0], _ = tied(middle_lows[0], pieces)
+            out_own, out_sent = out_weight_grads(
+                middle_lows, [state[3] for state in states], indices, blocks
+            )
+            hidden_kept = (*recompute(all_steps - 1, 1, out_own, hidden_kept), mlp_cols)
+            first_steps = all_steps // 2
+            *hidden_out, early_sums = hidden_grads(
+                upstream_rows, down_w, hidden_kept, indices, (gate_w, up_w), 0, first_steps
+            )
+            out_own, *hidden_out = tied(out_own, *hidden_out)
+            out_sum, *hidden_out = tied(added(out_own, out_sent), *hidden_out)
+            grad_out = lax.psum_scatter(
+                out_sum, "ctx", scatter_dimension=0, axis_index_groups=same_x
+            )
+            *hidden_out, late_sums = hidden_grads(
+                upstream_rows, down_w, hidden_kept, indices, (gate_w, up_w), first_steps,
+                all_steps - first_steps, hidden_out,
+            )
+            row_grads, *hidden_out = tied(row_grads, *hidden_out)
+        part_own, part_sent = heads_back(
+            row_grads, (in_hbm(query_w), *held[:2]), batches, indices, depth
+        )
+        part_other = other_core(part_sent)
+        if section == 0:
+            input_grads, grad_out = input_back(
+                part_own, part_other, middle_grad, section_in, gain_attn, indices, input_grads, grad_out
+            )
+        else:
+            input_grads, input_low = input_back(
+                part_own, part_other, middle_grad, section_in, gain_attn, indices, cotangent
+            )
+            arrived = lax.ppermute(input_low, "pipe", [(0, 1), (1, 0)])
+            *hidden_kept, mlp_cols = recompute(0, 1, input_low)
+            arrived, *hidden_kept = tied(arrived, *hidden_kept)
+    grad_query, grad_key, grad_value, gains = own_weight_grads(
+        row_grads, (query_w, key_w, value_w), (early_sums, late_sums), indices, depth
+    )
+    grad_gate, grad_up, grad_down = hidden_out
+    gains = jnp.sum(lax.all_gather(gains, "tp", axis=0), axis=0)
+    gains = gains / jnp.stack([owned_gain(gain_attn), owned_gain(gain_mlp)])
+    outs = (
+        section_out,
+        input_grads,
+        gains[0],
+        grad_query,
+        grad_key,
+        grad_value,
+        grad_out,
+        gains[1],
+        grad_gate,
+        grad_up,
+        grad_down,
+    )
+    return tuple(out[None] for out in outs)
+
+
 def solution(mesh):
     placed = (
         P(None, ("ctx", "tp"), None),
@@ -393,8 +1500,15 @@
         P("pipe", None, "tp"),
         P("pipe", None, "tp"),
     )
+
+    def chosen(*arrays):
+        batches, groups = arrays[0].shape[0], arrays[4].shape[-1] // HD
+        alike = batches == 2 and mesh.shape["ctx"] == batches * groups
+        alike = alike and mesh.shape["tp"] == 2 and mesh.shape["pipe"] == 2
+        return (on_device if alike else on_device_wide)(*arrays)
+
     return jax.shard_map(
-        on_device,
+        chosen,
         mesh=mesh,
         in_specs=placed,
         out_specs=(

time: 1520 us -> 445 us (0.29)
  waiting for transfers between devices: 707 us -> 109 us
  matrix products: 261 us -> 0 us
  blocking collectives: 256 us -> 31.8 us
  Pallas kernels: 0 us -> 211 us
  other arithmetic: 148 us -> 11.7 us
  local copies, waits for them, and re-layouts: 100 us -> 7.38 us
  starting transfers between devices: 18.9 us -> 51.9 us
    reduce_scatter x19 -> x1, waiting for transfers between devices: 520 us -> 0.01 us  [on_device(): lax.psum_scatter(out_sum, 'ctx', scatter_dimension=0, axis_index_groups=s...]
    dot_general x84 -> x0, matrix products: 261 us -> none  [the longest x21 94.3 us: dot_left_t(): lax.dot_general(left_op, right_op, (((0,), (0,)), ((), ())), preferred_el...]
    all_gather x18 -> x5, blocking collectives: 233 us -> 15.9 us  [the longest x4 13.8 us: tp_rows(): return lax.all_gather(part, 'tp', axis=1, tiled=True).reshape(rows, width)]
    pallas_call x0 -> x27, Pallas kernels: none -> 211 us  [the longest x6 86 us: stepped_call(): return lambda *arrays: call(indices, *arrays)]
    unnamed x25 -> x5, waiting for transfers between devices: 166 us -> 0.08 us
    select_n x32 -> x4, other arithmetic: 70.3 us -> 5.79 us  [the longest x2 3.16 us: here(): picked = jnp.where(section_at == section, value, picked)]
    all_to_all x0 -> x7, waiting for transfers between devices: none -> 59.1 us  [swap_blocks(): lax.all_to_all(pieces, 'ctx', split_axis=0, concat_axis=0, axis_index_gro...]
    ppermute x0 -> x12, waiting for transfers between devices: none -> 41.3 us  [the longest x8 15.5 us: other_core(): return lax.ppermute(array, 'tp', [(0, 1), (1, 0)])]
  transfers between devices with their start and end apart: 28 -> 25, of which waited for: 19 -> 16; matrix products, arithmetic and copies ran while one was open for 18% -> 3% of each run, Pallas kernels for 0% -> 41%
where the time goes in v1:
time: 445 us; the launch traced here: 438 us
  Pallas kernels  211 us (47%)
  waiting for transfers between devices  109 us (24%)
  starting transfers between devices  51.9 us (12%)
  blocking collectives  31.8 us (7%)
  between operations  14.7 us (3%)
  other arithmetic  11.7 us (3%)
  local copies, waits for them, and re-layouts  7.38 us (2%)
    pallas_call x6, Pallas kernels, stepped_call(): return lambda *arrays: call(indices, *arrays)  86 us
    all_to_all x7, waiting for transfers between devices, swap_blocks(): lax.all_to_all(pieces, 'ctx', split_axis=0, concat_axis=0, axis_index_gro...  59.1 us
    all_to_all x7, starting transfers between devices, swap_blocks(): lax.all_to_all(pieces, 'ctx', split_axis=0, concat_axis=0, axis_index_gro...  33.6 us
    pallas_call x2, Pallas kernels, feed_forward(): whole_call(body, tuple((pltpu.HBM(*shape) for shape in shapes)), scratch=...  25 us
    pallas_call x2, Pallas kernels, feed_forward_back(): whole_call(body, pltpu.HBM((rows, width), jnp.bfloat16), scratch=block_sc...  22 us
    all_to_all x1, blocking collectives, swap_blocks(): lax.all_to_all(pieces, 'ctx', split_axis=0, concat_axis=0, axis_index_gro...  15.9 us
    ppermute x8, waiting for transfers between devices, other_core(): return lax.ppermute(array, 'tp', [(0, 1), (1, 0)])  15.5 us
    pallas_call x2, Pallas kernels, attend_heads_back(): whole_call(body, pltpu.HBM(head_qkv.shape, jnp.bfloat16), scratch=[pltpu....  15.2 us
  transfers between devices with their start and end apart: 25, of which 16 were waited for; matrix products, arithmetic and copies ran while one was open for 3% of the time, Pallas kernels for 41%

profile of v1, /device:TPU:0, one launch (start us, length us, event | category | flops | bytes accessed | tf_op | source)
XLA Modules:
  0.0 438.1 jit_solution(6541413883099961875)
XLA Ops:
  17.4 7.1 %all-to-all-start = ((bf16[8,384,128]{2,1,0:T(8,128)(2,1)}), bf16[8,384,128]{2,1,0:T(8,128)(2,1)S(1)}, u32[]{:S(2)}, u32[]{:S(2)}) async-start(bf16[8,384,128]{2,1,0:T(8,128)(2,1)} %get-tuple-element.123), calls=%async_computation | async-start | bytes 1572864 | tf_op jit(solution)/shard_map/all_to_all | solution.py:1279
  37.7 7.5 %all-to-all-done.in_ref = bf16[8,384,128]{2,1,0:T(8,128)(2,1)S(1)} async-done(((bf16[8,384,128]{2,1,0:T(8,128)(2,1)}), bf16[8,384,128]{2,1,0:T(8,128)(2,1)S(1)}, u32[]{:S(2)}, u32[]{:S(2)}) %all-to-all-start) | async-done | bytes 786464 | tf_op jit(solution)/shard_map/all_to_all | solution.py:1279
  46.0 6.3 %shard_map.195 = (bf16[8,192,128]{2,1,0:T(8,128)(2,1)}, f32[2,1,1024]{2,1,0:T(1,128)}) custom-call(bf16[8,384,128]{2,1,0:T(8,128)(2,1)} %copy-done.13), custom_call_target="tpu_custom_call" | custom-call | flops 805306368 | bytes 2359296 | tf_op jit(solution)/shard_map/pallas_call | solution.py:574
  60.2 7.9 %all-to-all-done.1.in_ref = bf16[8,192,128]{2,1,0:T(8,128)(2,1)} async-done(((bf16[8,192,128]{2,1,0:T(8,128)(2,1)}), bf16[8,192,128]{2,1,0:T(8,128)(2,1)}, u32[]{:S(2)}, u32[]{:S(2)}) %all-to-all-start.1) | async-done | bytes 393248 | tf_op jit(solution)/shard_map/all_to_all | solution.py:1279
  73.4 12.7 %shard_map.198 = (f32[256,1536]{1,0:T(8,128)}, bf16[2,64,1536]{2,1,0:T(8,128)(2,1)}, bf16[256,2048]{1,0:T(8,128)(2,1)}, bf16[256,2048]{1,0:T(8,128)(2,1)}, bf16[...) custom-call(s32[4]{0:T(128)S(1)} %pad_add_fusion.at_ref._, bf16[256,1536]{1,0:T(8,128)(2,1)} %bitcast.74, ...), custom_call_target="tpu_custom_call" | custom-call | flops 4831838208 | bytes 18874368 | tf_op jit(solution)/shard_map/pallas_call | solution.py:828
  93.9 8.6 %collective-permute-done.3 = bf16[2,64,1536]{2,1,0:T(8,128)(2,1)S(1)} collective-permute-done((bf16[2,64,1536]{2,1,0:T(8,128)(2,1)S(1)}, bf16[2,64,1536]{2,1,0:T(8,128)(2,1)S(1)}, u32[]{:S(2)}, u32[]{:S(2)}) %collective-permute-start.3) | collective-permute-done | bytes 393248 | tf_op jit(solution)/shard_map/ppermute | solution.py:18
  117.8 8.5 %collective-permute-done.4 = bf16[128,1536]{1,0:T(8,128)(2,1)S(1)} collective-permute-done((bf16[128,1536]{1,0:T(8,128)(2,1)}, bf16[128,1536]{1,0:T(8,128)(2,1)S(1)}, u32[]{:S(2)}, u32[]{:S(2)}) %collective-permute-start.4) | collective-permute-done | bytes 393248 | tf_op jit(solution)/shard_map/ppermute | solution.py:1344
  128.2 6.5 %all-to-all-done.2.in_ref = bf16[8,384,128]{2,1,0:T(8,128)(2,1)} async-done(((bf16[8,384,128]{2,1,0:T(8,128)(2,1)}), bf16[8,384,128]{2,1,0:T(8,128)(2,1)}, u32[]{:S(2)}, u32[]{:S(2)}) %all-to-all-start.2) | async-done | bytes 786464 | tf_op jit(solution)/shard_map/all_to_all | solution.py:1279
  134.7 6.3 %shard_map.200 = (bf16[8,192,128]{2,1,0:T(8,128)(2,1)}, f32[2,1,1024]{2,1,0:T(1,128)}) custom-call(bf16[8,384,128]{2,1,0:T(8,128)(2,1)} %all-to-all-done.2.in_ref), custom_call_target="tpu_custom_call" | custom-call | flops 805306368 | bytes 2359296 | tf_op jit(solution)/shard_map/pallas_call | solution.py:574
  141.0 15.9 %all_to_all.40.in_ref = bf16[8,192,128]{2,1,0:T(8,128)(2,1)S(1)} all-to-all(bf16[8,192,128]{2,1,0:T(8,128)(2,1)} %get-tuple-element.149), channel_id=1, replica_groups=mesh['pipe'=2,'ctx'=8,'tp'=2] {'ctx'}, dimensions={0} | all-to-all | bytes 786432 | tf_op jit(solution)/shard_map/all_to_all | solution.py:1279
  161.4 12.3 %shard_map.202 = (f32[256,1536]{1,0:T(8,128)}, bf16[2,64,1536]{2,1,0:T(8,128)(2,1)}, bf16[256,2048]{1,0:T(8,128)(2,1)}, bf16[256,2048]{1,0:T(8,128)(2,1)}, bf16[...) custom-call(s32[4]{0:T(128)S(1)} %pad_add_fusion.at_ref._, bf16[256,1536]{1,0:T(8,128)(2,1)} %bitcast.77, ...), custom_call_target="tpu_custom_call" | custom-call | flops 4831838208 | bytes 18874368 | tf_op jit(solution)/shard_map/pallas_call | solution.py:828
  174.5 11.0 %shard_map.203.own_ref = bf16[256,1536]{1,0:T(8,128)(2,1)} custom-call(bf16[256,1536]{1,0:T(8,128)(2,1)} %bitcast.85, bf16[256,2048]{1,0:T(8,128)(2,1)} %get-tuple-element.151.gate_f_ref, bf16[256,2048]{1,0:T(8,128)(2,1)} %get-tuple-element.152.up_f_ref, bf16[1536,2048]{1,0:T(8,128)(2,1)} %bitcast.64, bf16[1536,2048]{1,0:T(8,128)(2,1)} %bitcast.46, ...), custom_call_target="tpu_custom_call" | custom-call | flops 4831838208 | bytes 18874368 | tf_op jit(solution)/shard_map/pallas_call | solution.py:866
  198.4 14.6 %all-to-all-done.4.grad_ref = bf16[8,192,128]{2,1,0:T(8,128)(2,1)} async-done(((bf16[8,192,128]{2,1,0:T(8,128)(2,1)}), bf16[8,192,128]{2,1,0:T(8,128)(2,1)}, u32[]{:S(2)}, u32[]{:S(2)}) %all-to-all-start.4) | async-done | bytes 393248 | tf_op jit(solution)/shard_map/all_to_all | solution.py:1279
  213.0 7.7 %shard_map.205.grad_1 = bf16[8,384,128]{2,1,0:T(8,128)(2,1)} custom-call(bf16[8,384,128]{2,1,0:T(8,128)(2,1)} %all-to-all-done.2.in_ref, bf16[8,192,128]{2,1,0:T(8,128)(2,1)} %all-to-all-done.4.grad_ref, f32[2,1,1024]{2,1,0:T(1,128)} %get-tuple-element.155.log_ref, f32[48,1024]{1,0:T(8,128)} %get-tuple-element.236.cos_ref, f32[48,1024]{1,0:T(8,128)} %get-tuple-element.235.sin_ref), custom_call_target="tpu_custom_call" | custom-call | flops 2013265920 | bytes 3145728 | tf_op jit(solution)/shard_map/pallas_call | solution.py:624
  229.3 22.7 %all-to-all-done.5.grad_ref = bf16[8,384,128]{2,1,0:T(8,128)(2,1)} async-done(((bf16[8,384,128]{2,1,0:T(8,128)(2,1)}), bf16[8,384,128]{2,1,0:T(8,128)(2,1)}, u32[]{:S(2)}, u32[]{:S(2)}) %all-to-all-start.5) | async-done | bytes 786464 | tf_op jit(solution)/shard_map/all_to_all | solution.py:1279
  266.4 12.7 %shard_map.208 = (bf16[2048,2048]{1,0:T(8,128)(2,1)}, bf16[2048,2048]{1,0:T(8,128)(2,1)}, bf16[2048,2048]{1,0:T(8,128)(2,1)}, bf16[192,2048]{1,0:T(8,128)(2,1)}) custom-call(s32[4]{0:T(128)S(1)} %pad_add_fusion.at_ref._, bf16[2048,1536]{1,0:T(8,128)(2,1)} %all-gather.9.cloned.1.call-done.all_ref, bf16[1536,2048]{1,0:T(8,128)(2,1)} %bitcast.47, ...), custom_call_target="tpu_custom_call" | custom-call | flops 6442450944 | bytes 15728640 | tf_op jit(solution)/shard_map/pallas_call | solution.py:692
  283.5 11.0 %shard_map.209.own_ref = bf16[256,1536]{1,0:T(8,128)(2,1)} custom-call(bf16[256,1536]{1,0:T(8,128)(2,1)} %bitcast.87, bf16[256,2048]{1,0:T(8,128)(2,1)} %get-tuple-element.174.gate_f_ref, bf16[256,2048]{1,0:T(8,128)(2,1)} %get-tuple-element.175.up_f_ref, bf16[1536,2048]{1,0:T(8,128)(2,1)} %bitcast.65, bf16[1536,2048]{1,0:T(8,128)(2,1)} %bitcast.48, ...), custom_call_target="tpu_custom_call" | custom-call | flops 4831838208 | bytes 18874368 | tf_op jit(solution)/shard_map/pallas_call | solution.py:866
  305.2 20.0 %shard_map.211 = (bf16[2048,2048]{1,0:T(8,128)(2,1)}, bf16[2048,2048]{1,0:T(8,128)(2,1)}, bf16[2048,2048]{1,0:T(8,128)(2,1)}) custom-call(s32[4]{0:T(128)S(1)} %pad_add_fusion.at_ref._, bf16[2048,1536]{1,0:T(8,128)(2,1)} %all-gather.9.cloned.1.call-done.all_ref, ...), custom_call_target="tpu_custom_call", output_to_operand_aliasing={{0}: (4, {}), {1}: (5, {}), {2}: (6, {})} | custom-call | flops 12884901888 | bytes 25165824 | tf_op jit(solution)/shard_map/pallas_call | solution.py:692
  325.2 7.5 %shard_map.212.grad_0 = bf16[8,384,128]{2,1,0:T(8,128)(2,1)} custom-call(bf16[8,384,128]{2,1,0:T(8,128)(2,1)} %copy-done.13, bf16[8,192,128]{2,1,0:T(8,128)(2,1)S(1)} %all-to-all-done.6.grad_ref, f32[2,1,1024]{2,1,0:T(1,128)} %get-tuple-element.185.log_ref, f32[48,1024]{1,0:T(8,128)} %get-tuple-element.236.cos_ref, f32[48,1024]{1,0:T(8,128)} %get-tuple-element.235.sin_ref), custom_call_target="tpu_custom_call" | custom-call | flops 2013265920 | bytes 3145728 | tf_op jit(solution)/shard_map/pallas_call | solution.py:624
  338.2 6.0 %all-to-all-start.7 = ((bf16[8,960,128]{2,1,0:T(8,128)(2,1)}), bf16[8,960,128]{2,1,0:T(8,128)(2,1)S(1)}, u32[]{:S(2)}, u32[]{:S(2)}) async-start(bf16[8,960,128]{2,1,0:T(8,128)(2,1)} %shard_map.213), calls=%async_computation.7 | async-start | bytes 3932160 | tf_op jit(solution)/shard_map/all_to_all | solution.py:1279
  350.5 12.4 %shard_map.215 = (bf16[2048,2048]{1,0:T(8,128)(2,1)}, bf16[2048,2048]{1,0:T(8,128)(2,1)}, bf16[2048,2048]{1,0:T(8,128)(2,1)}) custom-call(s32[4]{0:T(128)S(1)} %pad_add_fusion.at_ref._, bf16[2048,1536]{1,0:T(8,128)(2,1)} %all-gather.9.cloned.1.call-done.all_ref, ...), custom_call_target="tpu_custom_call", output_to_operand_aliasing={{0}: (4, {}), {1}: (5, {}), {2}: (6, {})} | custom-call | flops 6442450944 | bytes 15728640 | tf_op jit(solution)/shard_map/pallas_call | solution.py:692
  363.0 18.9 %shard_map.216 = (f32[192,2048]{1,0:T(8,128)}, f32[192,2048]{1,0:T(8,128)}, f32[192,2048]{1,0:T(8,128)}, f32[192,1]{1,0:T(8,128)}) custom-call(s32[4]{0:T(128)S(1)} %pad_add_fusion.at_ref._, bf16[2048,1536]{1,0:T(8,128)(2,1)} %all-gather.13.cloned.1.call-done.rows_ref, bf16[1536,2048]{1,0:T(8,128)(2,1)} %bitcast.66, ...), custom_call_target="tpu_custom_call" | custom-call | flops 8858370048 | bytes 22020096 | tf_op jit(solution)/shard_map/pallas_call | solution.py:692
  381.9 11.3 %collective-permute-done.11 = bf16[4,192,768]{2,1,0:T(8,128)(2,1)} collective-permute-done((bf16[4,192,768]{2,1,0:T(8,128)(2,1)}, bf16[4,192,768]{2,1,0:T(8,128)(2,1)}, u32[]{:S(2)}, u32[]{:S(2)}) %collective-permute-start.11) | collective-permute-done | bytes 1179680 | tf_op jit(solution)/shard_map/ppermute | solution.py:1357
  397.4 18.9 %shard_map.217 = (f32[192,2048]{1,0:T(8,128)}, f32[192,2048]{1,0:T(8,128)}, f32[192,2048]{1,0:T(8,128)}, f32[192,1]{1,0:T(8,128)}) custom-call(s32[4]{0:T(128)S(1)} %pad_add_fusion.at_ref._, bf16[2048,1536]{1,0:T(8,128)(2,1)} %all-gather.13.cloned.1.call-done.rows_ref, ...), custom_call_target="tpu_custom_call", output_to_operand_aliasing={{0}: (9, {}), {1}: (10, {}), {2}: (11, {})} | custom-call | flops 8858370048 | bytes 22020096 | tf_op jit(solution)/shard_map/pallas_call | solution.py:692
  (118 shorter events, 149.1 us)
Async XLA Ops:
  17.4 27.8 %all-to-all-start = ((bf16[8,384,128]{2,1,0:T(8,128)(2,1)}), bf16[8,384,128]{2,1,0:T(8,128)(2,1)S(1)}, u32[]{:S(2)}, u32[]{:S(2)}) async-start(bf16[8,384,128]{2,1,0:T(8,128)(2,1)} %get-tuple-element.123), calls=%async_computation | async-start | bytes 1572864 | tf_op jit(solution)/shard_map/all_to_all | solution.py:1279
  24.5 12.4 %collective-permute-start = (bf16[128,1536]{1,0:T(8,128)(2,1)}, bf16[128,1536]{1,0:T(8,128)(2,1)S(1)}, u32[]{:S(2)}, u32[]{:S(2)}) collective-permute-start(bf16[128,1536]{1,0:T(8,128)(2,1)} %get-tuple-element.125), channel_id=1, source_target_pairs={{0,2},{3,1},{4,6},{7,5},{8,10},{11,9},{12,14},{15,13},{16,18},{19,... | collective-permute-start | bytes 1179656 | tf_op jit(solution)/shard_map/ppermute | solution.py:1344
  52.3 15.7 %all-to-all-start.1 = ((bf16[8,192,128]{2,1,0:T(8,128)(2,1)}), bf16[8,192,128]{2,1,0:T(8,128)(2,1)}, u32[]{:S(2)}, u32[]{:S(2)}) async-start(bf16[8,192,128]{2,1,0:T(8,128)(2,1)} %get-tuple-element.129), calls=%async_computation.1 | async-start | bytes 786432 | tf_op jit(solution)/shard_map/all_to_all | solution.py:1279
  56.4 84.6 %all-gather.7.cloned.1.call-start = ((), (), s32[]{:S(2)}) async-start(), calls=%async_computation.9 | async-start | bytes 3538944 | tf_op jit(solution)/shard_map/all_gather | solution.py:1352
  70.8 2.6 collective-permute-start.1
  86.1 2.1 collective-permute-start.2
  90.5 12.0 %collective-permute-start.3 = (bf16[2,64,1536]{2,1,0:T(8,128)(2,1)S(1)}, bf16[2,64,1536]{2,1,0:T(8,128)(2,1)S(1)}, u32[]{:S(2)}, u32[]{:S(2)}) collective-permute-start(bf16[2,64,1536]{2,1,0:T(8,128)(2,1)S(1)} %add_convert_fusion.2), channel_id=1, source_target_pairs={{0,16},{1,17},{2,18},{3,19},{4,20},{5,21},{6,22},{7,23},{8,24},{9,... | collective-permute-start | bytes 1179656 | tf_op jit(solution)/shard_map/ppermute | solution.py:18
  109.8 24.9 %all-to-all-start.2 = ((bf16[8,384,128]{2,1,0:T(8,128)(2,1)}), bf16[8,384,128]{2,1,0:T(8,128)(2,1)}, u32[]{:S(2)}, u32[]{:S(2)}) async-start(bf16[8,384,128]{2,1,0:T(8,128)(2,1)} %get-tuple-element.142), calls=%async_computation.2 | async-start | bytes 1572864 | tf_op jit(solution)/shard_map/all_to_all | solution.py:1279
  114.0 152.3 %all-gather.9.cloned.1.call-start = ((), (), s32[]{:S(2)}) async-start(), calls=%async_computation.10 | async-start | bytes 6684672 | tf_op jit(solution)/shard_map/all_gather | solution.py:1340
  114.1 12.3 %collective-permute-start.4 = (bf16[128,1536]{1,0:T(8,128)(2,1)}, bf16[128,1536]{1,0:T(8,128)(2,1)S(1)}, u32[]{:S(2)}, u32[]{:S(2)}) collective-permute-start(bf16[128,1536]{1,0:T(8,128)(2,1)} %get-tuple-element.144), channel_id=1, source_target_pairs={{0,2},{3,1},{4,6},{7,5},{8,10},{11,9},{12,14},{15,13},{16,18},{19,... | collective-permute-start | bytes 1179656 | tf_op jit(solution)/shard_map/ppermute | solution.py:1344
  158.7 2.6 collective-permute-start.5
  185.5 2.6 collective-permute-start.6
  192.5 20.5 %all-to-all-start.4 = ((bf16[8,192,128]{2,1,0:T(8,128)(2,1)}), bf16[8,192,128]{2,1,0:T(8,128)(2,1)}, u32[]{:S(2)}, u32[]{:S(2)}) async-start(bf16[8,192,128]{2,1,0:T(8,128)(2,1)} %get-tuple-element.154), calls=%async_computation.4 | async-start | bytes 786432 | tf_op jit(solution)/shard_map/all_to_all | solution.py:1279
  196.8 135.9 %all-gather.11.cloned.1.call-start = ((), (), s32[]{:S(2)}) async-start(), calls=%async_computation.11 | async-start | bytes 3538944 | tf_op jit(solution)/shard_map/all_gather | solution.py:1352
  220.7 31.3 %all-to-all-start.5 = ((bf16[8,384,128]{2,1,0:T(8,128)(2,1)}), bf16[8,384,128]{2,1,0:T(8,128)(2,1)}, u32[]{:S(2)}, u32[]{:S(2)}) async-start(bf16[8,384,128]{2,1,0:T(8,128)(2,1)} %shard_map.205.grad_1), calls=%async_computation.5 | async-start | bytes 1572864 | tf_op jit(solution)/shard_map/all_to_all | solution.py:1279
  224.9 138.1 %all-gather.13.cloned.1.call-start = ((), (), s32[]{:S(2)}) async-start(), calls=%async_computation.12 | async-start | bytes 6684672 | tf_op jit(solution)/shard_map/all_gather | solution.py:1340
  224.9 2.0 collective-permute-start.7
  262.7 16.3 %collective-permute-start.9 = (bf16[2,64,1536]{2,1,0:T(8,128)(2,1)}, bf16[2,64,1536]{2,1,0:T(8,128)(2,1)}, u32[]{:S(2)}, u32[]{:S(2)}) collective-permute-start(bf16[2,64,1536]{2,1,0:T(8,128)(2,1)} %get-tuple-element.166), channel_id=1, source_target_pairs={{0,16},{16,0},{1,17},{17,1},{2,18},{18,2},{3,19},{19,3},{4,20},{20... | collective-permute-start | bytes 1179656 | tf_op jit(solution)/shard_map/ppermute | solution.py:1464
  294.5 2.6 collective-permute-start.10
  301.5 23.7 %all-to-all-start.6 = ((bf16[8,192,128]{2,1,0:T(8,128)(2,1)}), bf16[8,192,128]{2,1,0:T(8,128)(2,1)S(1)}, u32[]{:S(2)}, u32[]{:S(2)}) async-start(bf16[8,192,128]{2,1,0:T(8,128)(2,1)} %get-tuple-element.176), calls=%async_computation.6 | async-start | bytes 786432 | tf_op jit(solution)/shard_map/all_to_all | solution.py:1279
  338.2 78.1 %all-to-all-start.7 = ((bf16[8,960,128]{2,1,0:T(8,128)(2,1)}), bf16[8,960,128]{2,1,0:T(8,128)(2,1)S(1)}, u32[]{:S(2)}, u32[]{:S(2)}) async-start(bf16[8,960,128]{2,1,0:T(8,128)(2,1)} %shard_map.213), calls=%async_computation.7 | async-start | bytes 3932160 | tf_op jit(solution)/shard_map/all_to_all | solution.py:1279
  344.2 83.5 %reduce-scatter.2.cloned.1.call-start = ((), (), s32[]{:S(2)}) async-start(), calls=%async_computation.13 | async-start | bytes 1474560 | tf_op jit(solution)/shard_map/reduce_scatter | solution.py:1444
  348.5 44.7 %collective-permute-start.11 = (bf16[4,192,768]{2,1,0:T(8,128)(2,1)}, bf16[4,192,768]{2,1,0:T(8,128)(2,1)}, u32[]{:S(2)}, u32[]{:S(2)}) collective-permute-start(bf16[4,192,768]{2,1,0:T(8,128)(2,1)} %get-tuple-element.208), channel_id=1, source_target_pairs={{0,2},{2,0},{4,6},{6,4},{8,10},{10,8},{12,14},{14,12},{1,3},{3,1},... | collective-permute-start | bytes 3538952 | tf_op jit(solution)/shard_map/ppermute | solution.py:1357
  421.9 5.7 %collective-permute-start.12 = (bf16[2,64,1536]{2,1,0:T(8,128)(2,1)}, bf16[2,64,1536]{2,1,0:T(8,128)(2,1)S(1)}, u32[]{:S(2)}, u32[]{:S(2)}) collective-permute-start(bf16[2,64,1536]{2,1,0:T(8,128)(2,1)} %get-tuple-element.220), channel_id=1, source_target_pairs={{0,1},{1,0},{2,3},{3,2},{4,5},{5,4},{6,7},{7,6},{8,9},{9,8},{10,11... | collective-permute-start | bytes 1179656 | tf_op jit(solution)/shard_map/ppermute | solution.py:1285
  (17 other events, 164.1 us)
Sparse Core Ops, SparseCore 0:
  70.9 37.3 all-gather.6
  174.6 75.9 all-gather.8
  252.2 34.8 all-gather.10
  289.3 72.2 all-gather.12
  396.0 28.1 reduce-scatter.1
